TPU v7x, 256 devices: a whole 4x4x8 slice. The times are simulated.
256 devices in a mesh: clip: 2 (over y_lo), seq: 128 (over y_hi, x, z, core).
Axes of the slice: x: 4, y: 4 (y_hi: 2, y_lo: 2; y = y_hi * 2 + y_lo), z: 8, core: 2. Of those that a mesh axis runs over, the one named last changes fastest.
Arguments:
- clips_x: bfloat16 [8, 32768, 1280], P('clip', 'seq'), parts along dimension 0, may hold values from -6 to 6
- slot_phi: bfloat16 [1280, 256], replicated, may hold values from -38.572173 to 38.572173
- w_in: bfloat16 [1280, 163840], P(None, 'seq'), may hold values from -0.875 to 0.875
- b_in: bfloat16 [163840], P('seq'), may hold values from -1.5 to 1.5
- w_out: bfloat16 [163840, 1280], P('seq'), may hold values from -0.125 to 0.125
- b_out: bfloat16 [64, 1280], replicated, may hold values from -1.5 to 1.5
Outputs:
- mixed: bfloat16 [8, 32768, 1280], P('clip', 'seq'), parts along dimension 0
There are 2 independent parts, one for each index of `clip`. A program takes and returns all parts, laid end to end along the dimension named above; an argument that names none is the same for every part. Nothing has to cross between parts.
All inputs are finite; a program needn't handle non-finite values.
Results may differ from a plain program's by a relative error of at most 0.014.
Values may be sent and summed in bfloat16 or wider, within the bound.
No kernel may reach another device: no remote copies, remote signals or barrier semaphores. Data moves between devices by JAX's collectives and lax.ppermute only.
A program may use at most 128 MiB of HBM per device.

v0:
```python
import jax
import jax.numpy as jnp
from jax import lax
from jax.sharding import PartitionSpec as P


def swapped(value, axis, distance):
    mask = 2**distance
    pairs = [(source, source ^ mask) for source in range(lax.axis_size(axis))]
    return lax.ppermute(value, axis, pairs)


def scatter_slots(dispatch, clips_x):
    return lax.psum_scatter(
        jnp.einsum("ctj,ctd->jcd", dispatch, clips_x, preferred_element_type=jnp.float32),
        "seq",
        scatter_dimension=0,
        tiled=True,
    )


def per_device(clips_x, slot_phi, w_in, b_in, w_out, b_out):
    slots_all = slot_phi.shape[1]
    owned = slots_all // lax.axis_size("seq")
    me = lax.axis_index("seq")
    parity = me % 2
    logits = jnp.einsum("ctd,dj->ctj", clips_x, slot_phi, preferred_element_type=jnp.float32)
    local_max = jnp.max(logits, axis=1)
    col_max = lax.pmax(local_max, "seq")
    expo = jnp.exp(logits - col_max[:, None, :])
    col_total = lax.psum(jnp.sum(expo, axis=1), "seq")
    dispatch = expo.astype(jnp.bfloat16)
    numer_own = scatter_slots(dispatch, clips_x)
    total_own = lax.dynamic_slice_in_dim(col_total, me * owned, owned, 1).T
    slot_in = (numer_own / total_own[:, :, None]).astype(jnp.bfloat16)
    bias_out = lax.dynamic_slice_in_dim(b_out, me // 2, 1, 0).astype(jnp.float32)
    partner = swapped(slot_in, "seq", 0)
    leading = jnp.where(parity == 0, slot_in, partner)
    trailing = jnp.where(parity == 0, partner, slot_in)
    expert_rows = jnp.concatenate([leading, trailing], axis=0)
    pre = jnp.einsum("scd,df->scf", expert_rows, w_in, preferred_element_type=jnp.float32)
    hidden = jax.nn.gelu(pre + b_in.astype(jnp.float32), approximate=False).astype(jnp.bfloat16)
    partial_out = jnp.einsum("scf,fd->scd", hidden, w_out, preferred_element_type=jnp.float32)
    head = partial_out[:owned]
    tail = partial_out[owned:]
    mine = jnp.where(parity == 0, head, tail)
    theirs = jnp.where(parity == 0, tail, head)
    summed = mine + swapped(theirs.astype(jnp.bfloat16), "seq", 0).astype(theirs.dtype)
    slot_out = (summed + bias_out[None]).astype(jnp.bfloat16)
    row_max = jnp.max(logits, axis=2, keepdims=True)
    weights = jnp.exp(logits - row_max)
    comb = (weights / jnp.sum(weights, axis=2, keepdims=True)).astype(jnp.bfloat16)
    mixed = jnp.einsum(
        "ctj,jcd->ctd",
        comb,
        lax.all_gather(slot_out, "seq", axis=0, tiled=True),
        preferred_element_type=jnp.float32,
    )
    return mixed.astype(jnp.bfloat16)


def solution(mesh):
    placed = (P("clip", "seq", None), P(), P(None, "seq"), P("seq"), P("seq", None), P())
    return jax.shard_map(
        per_device, mesh=mesh, in_specs=placed, out_specs=P("clip", "seq", None), check_vma=False
    )
```

profile of v0, /device:TPU:1, one launch (start us, length us, event | category | flops | bytes accessed | tf_op | source)
XLA Modules:
  0.0 1757.2 jit_solution(4353197108701877813)
XLA Ops:
  6.5 3.9 fusion.99
  10.4 327.9 %pmax.7 = f32[4,256]{1,0:T(4,128)S(1)} all-reduce(f32[4,256]{1,0:T(4,128)S(1)} %get-tuple-element.9), channel_id=1, replica_groups=mesh['clip'=2,'seq'=128] {'seq'}, use_global_device_ids=true, to_apply=%region_3.4 | all-reduce | flops 1024 | bytes 8192 | tf_op jit(solution)/shard_map/pmax | solution.py:29
  338.3 3.0 convolution_bitcast_fusion
  341.3 5.7 copy.15
  347.0 0.0 all-gather.2.cloned.1.call-start
  347.1 1.4 fusion.11
  348.4 330.5 %psum.7 = f32[4,256]{1,0:T(4,128)S(1)} all-reduce(f32[4,256]{1,0:T(4,128)S(1)} %fusion.11), channel_id=1, replica_groups=mesh['clip'=2,'seq'=128] {'seq'}, use_global_device_ids=true, to_apply=%region_6.7 | all-reduce | flops 1024 | bytes 8192 | tf_op jit(solution)/shard_map/psum | solution.py:31
  679.0 0.1 dynamic-slice_bitcast_fusion
  679.0 0.1 copy.16
  679.1 0.6 dynamic-slice
  680.4 942.7 %all-reduce.3.cloned.1.call-done = f32[256,4,1280]{2,1,0:T(4,128)} async-done(((f32[256,4,1280]{2,1,0:T(4,128)}), f32[256,4,1280]{2,1,0:T(4,128)}) %all-reduce.3.cloned.1.call-update) | async-done | bytes 5242896
  1623.0 0.9 fusion.61
  1623.9 7.1 collective-permute-start
  1631.0 0.8 collective-permute-done
  1631.9 1.0 broadcast_select_fusion.1
  1632.9 0.6 fusion.63
  1633.6 0.9 fusion.1
  1634.4 0.3 collective-permute-start.1
  1634.7 0.7 convert_reduce_fusion
  1635.5 0.2 collective-permute-done.1
  1635.7 0.6 add_convert_fusion
  1636.4 1.9 fusion.100
  1638.3 106.0 %all-gather.2.cloned.1.call-done = bf16[256,4,1280]{2,1,0:T(4,128)(2,1)} async-done(((bf16[2,4,1280]{2,1,0:T(4,128)(2,1)}), bf16[256,4,1280]{2,1,0:T(4,128)(2,1)}) %all-gather.2.cloned.1.call-update) | async-done | bytes 2621456 | tf_op jit(solution)/shard_map/all_gather | solution.py:56
  1744.3 6.1 convolution_convert_fusion
  (13 shorter events, 0.1 us)
Async XLA Ops:
  6.5 1626.4 %copy-start = (bf16[1280,1280]{1,0:T(8,128)(2,1)S(1)}, bf16[1280,1280]{1,0:T(8,128)(2,1)}, u32[]{:S(2)}) copy-start(bf16[1280,1280]{1,0:T(8,128)(2,1)} %param.8) | copy-start | bytes 9830404
  6.5 1616.5 %all-reduce.3.cloned.1.call-start = ((), (), s32[]{:S(2)}) async-start(), calls=%async_computation.1 | async-start | bytes 10485760
  347.0 332.2 %copy-start.3 = (u32[256]{0:T(256)S(1)}, u32[256]{0:T(256)}, u32[]{:S(2)}) copy-start(u32[256]{0:T(256)} %constant.98) | copy-start | bytes 3076
  347.0 1284.1 %copy-start.1 = (bf16[1280]{0:T(1024)(128)(2,1)S(1)}, bf16[1280]{0:T(1024)(128)(2,1)}, u32[]{:S(2)}) copy-start(bf16[1280]{0:T(1024)(128)(2,1)} %param.9) | copy-start | bytes 7684
  347.0 1397.3 %all-gather.2.cloned.1.call-start = ((), (), s32[]{:S(2)}) async-start(), calls=%async_computation | async-start | bytes 2641920 | tf_op jit(solution)/shard_map/all_gather | solution.py:56
  1623.9 8.0 collective-permute-start
  1631.0 2.5 copy-start.2
  1634.4 1.3 collective-permute-start.1
Sparse Core Ops, SparseCore 0:
  347.1 1275.8 all-reduce.2
  1636.5 107.7 all-gather.1
where the time goes:
time: 1760 us
  waiting for transfers between devices  1050 us (60%)
  blocking collectives  658 us (37%)
    unnamed x3, waiting for transfers between devices  943 us
    psum x1, blocking collectives, per_device(): col_total = lax.psum(jnp.sum(expo, axis=1), 'seq')  331 us
    pmax x1, blocking collectives, per_device(): col_max = lax.pmax(local_max, 'seq')  328 us
    all_gather x1, waiting for transfers between devices, per_device(): lax.all_gather(slot_out, 'seq', axis=0, tiled=True)  106 us
  transfers between devices with their start and end apart: 4, of which 4 were waited for; matrix products, arithmetic and copies ran while one was open for 0% of the time, Pallas kernels for 0%

commit v1 on v0

v1 whole, which is shorter than its diff:
```python
import jax
import jax.numpy as jnp
from jax import lax
from jax.sharding import PartitionSpec as P

LANES = 128


def coords(index):
    return index // 64, index // 16 % 4, index // 2 % 8, index % 2


def groups_by(key):
    found = {}
    for index in range(128):
        found.setdefault(key(*coords(index)), []).append(index)
    return list(found.values())


ALONG_X = groups_by(lambda y, x, z, core: (y, z, core))
ALONG_YZ = groups_by(lambda y, x, z, core: (x, core))


def exchange(value, groups):
    return lax.all_to_all(value, "seq", 0, 0, tiled=True, axis_index_groups=groups)


def swap_cores(value):
    return lax.ppermute(value, "seq", [(source, source ^ 1) for source in range(128)])


def short(value):
    return lax.reduce_precision(value, 8, 7)


def with_stats(numer, peak, total):
    p1 = short(peak)
    p2 = short(peak - p1)
    p3 = peak - p1 - p2
    t1 = short(total)
    t2 = total - t1
    pad = jnp.zeros(peak.shape[:-1] + (LANES - 5,), jnp.float32)
    return jnp.concatenate([numer, p1, p2, p3, t1, t2, pad], axis=-1).astype(jnp.bfloat16)


def stats_of(packed):
    s = packed[..., -LANES:].astype(jnp.float32)
    return s[..., 0:1] + s[..., 1:2] + s[..., 2:3], s[..., 3:4] + s[..., 4:5]


def merged(packed):
    peaks, totals = stats_of(packed)
    peak = jnp.max(peaks, axis=0)
    factor = jnp.exp(peaks - peak)
    total = jnp.sum(factor * totals, axis=0)
    numer = jnp.sum(factor * packed[..., :-LANES].astype(jnp.float32), axis=0)
    return numer, peak, total


def per_device(clips_x, slot_phi, w_in, b_in, w_out, b_out):
    clips, tokens, width = clips_x.shape
    half = width // 2
    me = lax.axis_index("seq")
    core = me % 2
    mine = core * half
    theirs = half - mine
    logits = jnp.einsum("dj,ctd->cjt", slot_phi, clips_x, preferred_element_type=jnp.float32)
    peak = jnp.max(logits, axis=2, keepdims=True)
    expo = jnp.exp(logits - peak)
    total = jnp.sum(expo, axis=2, keepdims=True)
    dispatch = expo.astype(jnp.bfloat16)

    def sums(start):
        part = lax.dynamic_slice_in_dim(clips_x, start, half, 2)
        return jnp.einsum("cjt,ctd->cjd", dispatch, part, preferred_element_type=jnp.float32)

    arrived = swap_cores(with_stats(sums(theirs), peak, total))
    own = sums(mine)
    other_peak, other_total = stats_of(arrived)
    top = jnp.maximum(peak, other_peak)
    f_own = jnp.exp(peak - top)
    f_other = jnp.exp(other_peak - top)
    numer = f_own * own + f_other * arrived[..., :-LANES].astype(jnp.float32)
    packed = with_stats(numer, top, f_own * total + f_other * other_total)
    packed = packed.reshape(clips, 2, 4, 32, half + LANES).transpose(2, 0, 1, 3, 4)
    packed = exchange(packed.reshape(4, clips * 64, half + LANES), ALONG_X)
    packed = with_stats(*merged(packed.reshape(4, clips * 64, half + LANES)))
    packed = packed.reshape(clips, 16, 4, half + LANES).transpose(1, 0, 2, 3)
    packed = exchange(packed.reshape(16, clips * 4, half + LANES), ALONG_YZ)
    numer, _, total = merged(packed)
    slot_in = (numer / total).astype(jnp.bfloat16)
    partner = swap_cores(slot_in)
    rows = jnp.where(
        core == 0,
        jnp.concatenate([slot_in, partner], axis=1),
        jnp.concatenate([partner, slot_in], axis=1),
    )
    pre = jnp.dot(rows, w_in, preferred_element_type=jnp.float32)
    hidden = jax.nn.gelu(pre + b_in.astype(jnp.float32), approximate=False).astype(jnp.bfloat16)
    partial = jnp.dot(hidden, w_out, preferred_element_type=jnp.float32)
    part_mine = jnp.where(core == 0, partial[:, :half], partial[:, half:])
    part_theirs = jnp.where(core == 0, partial[:, half:], partial[:, :half])
    bias = lax.dynamic_slice(b_out, (me // 2, mine), (1, half)).astype(jnp.float32)
    summed = part_mine + swap_cores(part_theirs.astype(jnp.bfloat16)).astype(jnp.float32)
    slot_out = (summed + bias).astype(jnp.bfloat16)
    gathered = exchange(jnp.broadcast_to(slot_out[None], (16,) + slot_out.shape), ALONG_YZ)
    gathered = gathered.reshape(16, clips, 4, half).transpose(1, 0, 2, 3).reshape(1, clips * 64, half)
    gathered = exchange(jnp.broadcast_to(gathered, (4, clips * 64, half)), ALONG_X)
    gathered = gathered.reshape(4, clips, 2, 32, half).transpose(1, 2, 0, 3, 4).reshape(clips, 256, half)
    other = swap_cores(gathered)
    row_max = jnp.max(logits, axis=1, keepdims=True)
    weights = jnp.exp(logits - row_max)
    comb = (weights / jnp.sum(weights, axis=1, keepdims=True)).astype(jnp.bfloat16)

    def mix(values):
        return jnp.einsum("cjt,cjd->ctd", comb, values, preferred_element_type=jnp.float32).astype(jnp.bfloat16)

    a, b = mix(gathered), mix(other)
    return jnp.where(core == 0, jnp.concatenate([a, b], axis=2), jnp.concatenate([b, a], axis=2))


def solution(mesh):
    placed = (P("clip", "seq", None), P(), P(None, "seq"), P("seq"), P("seq", None), P())
    return jax.shard_map(
        per_device, mesh=mesh, in_specs=placed, out_specs=P("clip", "seq", None), check_vma=False
    )
```

time: 1760 us -> 182 us (0.10)
  waiting for transfers between devices: 1050 us -> 0.9 us
  blocking collectives: 658 us -> 79.4 us
  local copies, waits for them, and re-layouts: 6.49 us -> 45 us
    unnamed x3 -> x0, waiting for transfers between devices: 943 us -> none
    psum x1 -> x0, blocking collectives: 331 us -> none  [per_device(): col_total = lax.psum(jnp.sum(expo, axis=1), 'seq')]
    pmax x1 -> x0, blocking collectives: 328 us -> none  [per_device(): col_max = lax.pmax(local_max, 'seq')]
    all_gather x1 -> x0, waiting for transfers between devices: 106 us -> none  [per_device(): lax.all_gather(slot_out, 'seq', axis=0, tiled=True)]
    all_to_all x0 -> x4, blocking collectives: none -> 79.4 us  [exchange(): lax.all_to_all(value, 'seq', 0, 0, tiled=True, axis_index_groups=groups)]
  transfers between devices with their start and end apart: 4 -> 4, of which waited for: 4 -> 2; matrix products, arithmetic and copies ran while one was open for 0% -> 8% of each run, Pallas kernels for 0% -> 0%
where the time goes in v1:
time: 182 us; the launch traced here: 181 us
  blocking collectives  79.4 us (44%)
  local copies, waits for them, and re-layouts  45 us (25%)
  matrix products  23.9 us (13%)
  other arithmetic  21.2 us (12%)
  starting transfers between devices  10 us (5%)
    all_to_all x4, blocking collectives, exchange(): lax.all_to_all(value, 'seq', 0, 0, tiled=True, axis_index_groups=groups)  79.4 us
    concatenate x10, local copies, waits for them, and re-layouts, with_stats(): jnp.concatenate([numer, p1, p2, p3, t1, t2, pad], axis=-1)  16.9 us
    dot_general x2, matrix products, mix(): jnp.einsum('cjt,cjd->ctd', comb, values, preferred_element_type=jnp.float32)  10.1 us
    ppermute x4, starting transfers between devices, swap_cores(): lax.ppermute(value, 'seq', [(source, source ^ 1) for source in range(128)])  10 us
    dot_general x2, local copies, waits for them, and re-layouts, sums(): jnp.einsum('cjt,ctd->cjd', dispatch, part, preferred_element_type=jnp.flo...  7.59 us
    dot_general x2, matrix products, sums(): jnp.einsum('cjt,ctd->cjd', dispatch, part, preferred_element_type=jnp.flo...  6.77 us
    unnamed x19, local copies, waits for them, and re-layouts  5.57 us
    another operation x6, local copies, waits for them, and re-layouts  5.06 us
  transfers between devices with their start and end apart: 4, of which 2 were waited for; matrix products, arithmetic and copies ran while one was open for 8% of the time, Pallas kernels for 0%

profile of v1, /device:TPU:1, one launch (start us, length us, event | category | flops | bytes accessed | tf_op | source)
XLA Modules:
  0.0 180.5 jit_solution(7359379633166785615)
XLA Ops:
  0.0 3.9 %fusion.120 = (f32[4,256]{1,0:T(4,128)S(1)}, f32[4,256,256]{1,2,0:T(8,128)}) fusion(bf16[4,256,1280]{2,1,0:T(8,128)(2,1)} %param.6, bf16[1280,256]{1,0:T(8,128)(2,1)} %param.7), kind=kOutput, calls=%fused_computation.176 | convolution fusion | flops 671349760 | bytes 4329472 | tf_op jit(solution)/shard_map/dj,ctd->cjt/dot_general | solution.py:67
  5.4 3.0 %fusion.5 = bf16[4,256,640]{2,1,0:T(8,128)(2,1)} fusion(bf16[4,256,1280]{2,1,0:T(8,128)(2,1)} %param.6, s32[]{:T(128)S(6)} %select_n.53, f32[4,256,256]{1,2,0:T(8,128)S(1)} %copy-done.2, f32[4,256]{1,0:T(4,128)S(1)} %get-tuple-element.26), kind=kOutput, calls=%fused_computation.13 | convolution fusion | flops 336068608 | bytes 3674116 | tf_op jit(solution)/shard_map/cjt,ctd->cjd/dot_general | solution.py:75
  8.4 3.4 %copy.112 = bf16[4,256,640]{1,0,2:T(4,128)(2,1)} copy(bf16[4,256,640]{2,1,0:T(8,128)(2,1)} %fusion.5) | data formatting | bytes 2621440 | tf_op jit(solution)/shard_map/cjt,ctd->cjd/dot_general | solution.py:75
  11.9 2.8 %convert_dynamic-update-slice_fusion = bf16[4,256,768]{1,0,2:T(4,128)(2,1)} fusion(bf16[4,256,640]{1,0,2:T(4,128)(2,1)} %copy.112), kind=kLoop, calls=%fused_computation.12 | loop fusion | bytes 2621440
  18.4 3.2 %collective-permute-start = (bf16[4,256,768]{1,0,2:T(4,128)(2,1)}, bf16[4,256,768]{1,0,2:T(4,128)(2,1)}, u32[]{:S(2)}, u32[]{:S(2)}) collective-permute-start(bf16[4,256,768]{1,0,2:T(4,128)(2,1)} %broadcast_dynamic-update-slice_fusion), channel_id=1, source_target_pairs={{0,1},{1,0},{2,3},{3,2},{4,5},{5,4},{6,7},{7,6},{8,9},{9,8},{10,11... | collective-permute-start | bytes 4718600 | tf_op jit(solution)/shard_map/ppermute | solution.py:29
  21.6 3.8 %fusion.3 = f32[4,256,640]{2,1,0:T(8,128)} fusion(bf16[4,256,1280]{2,1,0:T(8,128)(2,1)} %param.6, s32[]{:T(128)S(6)} %select_n.54, f32[4,256,256]{1,2,0:T(8,128)} %get-tuple-element.27, f32[4,256]{1,0:T(4,128)S(1)} %get-tuple-element.26), kind=kOutput, calls=%fused_computation.10 | convolution fusion | flops 336068608 | bytes 4984836 | tf_op jit(solution)/shard_map/cjt,ctd->cjd/dot_general | solution.py:75
  25.4 4.2 %copy.114 = f32[4,256,640]{1,0,2:T(4,128)} copy(f32[4,256,640]{2,1,0:T(8,128)} %fusion.3) | data formatting | bytes 5242880 | tf_op jit(solution)/shard_map/cjt,ctd->cjd/dot_general | solution.py:75
  31.2 4.0 %add_convert_fusion = bf16[4,256,640]{1,0,2:T(4,128)(2,1)} fusion(f32[4,256,640]{1,0,2:T(4,128)} %copy.114, bf16[4,256,768]{1,0,2:T(4,128)(2,1)} %collective-permute-done, f32[4,256]{1,0:T(4,128)S(1)} %get-tuple-element.24, f32[4,256]{1,0:T(4,128)S(1)} %get-tuple-element.25), kind=kLoop, calls=%fused_computation.3 | loop fusion | flops 3276800 | bytes 5251072 | tf_op jit(solution)/shard_map/convert.21
  35.2 3.5 %copy.115 = bf16[4,256,640]{2,1,0:T(8,128)(2,1)} copy(bf16[4,256,640]{1,0,2:T(4,128)(2,1)} %add_convert_fusion) | data formatting | bytes 2621440 | tf_op jit(solution)/shard_map/convert.21
  42.6 1.8 %concatenate.61 = bf16[4,2,4,32,1]{4,3,2,1,0:T(8,128)(2,1)} reshape(bf16[4,256,1]{1,0,2:T(4,128)(2,1)} %get-tuple-element.11) | data formatting | bytes 4096 | tf_op jit(solution)/shard_map/concatenate | solution.py:43
  45.2 4.5 %concatenate.50 = bf16[4,2,4,32,768]{4,3,2,1,0:T(8,128)(2,1)} concatenate(bf16[4,2,4,32,640]{4,3,2,1,0:T(8,128)(2,1)} %bitcast.91, bf16[4,2,4,32,1]{4,3,2,1,0:T(8,128)(2,1)S(1)} %concatenate.57, bf16[4,2,4,32,1]{4,3,2,1,0:T(8,128)(2,1)} %concatenate.58, bf16[4,2,4,32,1]{4,3,2,1,0:T(8,128)(2,1)} %concatenate.59, bf16[4,2,4,32,1]{4,3,2,1,0:T(8,128)(2,1)} %concatenate.60, ...), dimensions={4} | concatenate | bytes 3145728 | tf_op jit(solution)/shard_map/concatenate | solution.py:43
  51.3 23.0 %all_to_all.20 = bf16[4,256,768]{2,1,0:T(8,128)(2,1)S(1)} all-to-all(bf16[4,256,768]{2,1,0:T(8,128)(2,1)S(1)} %bitcast.89), channel_id=1, replica_groups={{0,16,32,48},{1,17,33,49},{2,18,34,50},{3,19,35,51},{4,20,36,52},{5,21,..., dimensions={0} | all-to-all | bytes 3145728 | tf_op jit(solution)/shard_map/all_to_all | solution.py:25
  77.5 2.1 %fusion.11 = (f32[256]{0:T(256)S(1)}, f32[4,256]{1,0:T(4,128)S(1)}) fusion(f32[4,256,128]{2,1,0:T(8,128)} %copy-done.1, f32[4,256,1]{2,1,0:T(8,128)} %get-tuple-element.10, f32[256]{0:T(256)S(1)} %get-tuple-element.9), kind=kLoop, calls=%fused_computation.23 | loop fusion | flops 3840 | bytes 18432 | tf_op jit(solution)/shard_map/reduce_sum | solution.py:55
  80.7 1.8 concatenate.51
  85.0 3.3 %concatenate.52 = bf16[4,16,4,768]{3,2,1,0:T(4,128)(2,1)} concatenate(bf16[4,16,4,640]{3,2,1,0:T(4,128)(2,1)} %concatenate.51, bf16[4,16,4,1]{3,2,1,0:T(4,128)(2,1)S(1)} %copy.126, bf16[4,16,4,1]{3,2,1,0:T(4,128)(2,1)S(1)} %copy.127, bf16[4,16,4,1]{3,2,1,0:T(4,128)(2,1)S(1)} %copy.128, bf16[4,16,4,1]{3,2,1,0:T(4,128)(2,1)S(1)} %copy.129, bf16[4,16,4,1]{3,2,1,0:T(4,128)(2,1)} %copy.130, ...), dimensions={3} | concatenate | bytes 786432 | tf_op jit(solution)/shard_map/concatenate | solution.py:43
  89.4 22.6 %all_to_all.21 = bf16[16,16,768]{2,1,0:T(8,128)(2,1)S(1)} all-to-all(bf16[16,16,768]{2,1,0:T(8,128)(2,1)S(1)} %copy.132), channel_id=1, replica_groups={{0,2,4,6,8,10,12,14,64,66,68,70,72,74,76,78},{1,3,5,7,9,11,13,15,65,67,..., dimensions={0} | all-to-all | bytes 786432 | tf_op jit(solution)/shard_map/all_to_all | solution.py:25
  115.4 3.0 %collective-permute-start.1 = (bf16[16,640]{1,0:T(8,128)(2,1)S(1)}, bf16[16,640]{1,0:T(8,128)(2,1)S(1)}, u32[]{:S(2)}, u32[]{:S(2)}) collective-permute-start(bf16[16,640]{1,0:T(8,128)(2,1)S(1)} %divide_convert_fusion.1), channel_id=1, source_target_pairs={{0,1},{1,0},{2,3},{3,2},{4,5},{5,4},{6,7},{7,6},{8,9},{9,8},{10,11... | collective-permute-start | bytes 61448 | tf_op jit(solution)/shard_map/ppermute | solution.py:29
  119.3 3.1 %fusion.25 = f32[16,1280]{1,0:T(8,128)S(1)} fusion(bf16[1280,1280]{1,0:T(8,128)(2,1)S(1)} %copy-done, bf16[1280,1280]{1,0:T(8,128)(2,1)} %param.8, bf16[16,640]{1,0:T(8,128)(2,1)S(1)} %collective-permute-done.1, bf16[16,640]{1,0:T(8,128)(2,1)S(1)} %divide_convert_fusion.1, f32[1280]{0:T(1024)S(1)} %convert_element_type.63, pred[]{:T(512)S(6)} %eq.4), kind=kOutput, calls=%fused_computation.50 | convolution fusion | flops 106393600 | bytes 6681601 | tf_op jit(solution)/shard_map/dot_general | solution.py:100
  123.7 15.7 %all_to_all.22 = bf16[16,16,640]{2,1,0:T(8,128)(2,1)S(1)} all-to-all(bf16[16,16,640]{2,1,0:T(8,128)(2,1)S(1)} %broadcast_in_dim.12), channel_id=1, replica_groups={{0,2,4,6,8,10,12,14,64,66,68,70,72,74,76,78},{1,3,5,7,9,11,13,15,65,67,..., dimensions={0} | all-to-all | bytes 655360 | tf_op jit(solution)/shard_map/all_to_all | solution.py:25
  143.2 18.0 %all_to_all.23 = bf16[4,256,640]{2,1,0:T(8,128)(2,1)S(1)} all-to-all(bf16[4,256,640]{2,1,0:T(8,128)(2,1)S(1)} %broadcast_in_dim.14), channel_id=1, replica_groups={{0,16,32,48},{1,17,33,49},{2,18,34,50},{3,19,35,51},{4,20,36,52},{5,21,..., dimensions={0} | all-to-all | bytes 2621440 | tf_op jit(solution)/shard_map/all_to_all | solution.py:25
  162.4 3.3 %collective-permute-start.3 = (bf16[4,256,640]{2,1,0:T(8,128)(2,1)}, bf16[4,256,640]{2,1,0:T(8,128)(2,1)}, u32[]{:S(2)}, u32[]{:S(2)}) collective-permute-start(bf16[4,256,640]{2,1,0:T(8,128)(2,1)} %bitcast.16), channel_id=1, source_target_pairs={{0,1},{1,0},{2,3},{3,2},{4,5},{5,4},{6,7},{7,6},{8,9},{9,8},{10,11... | collective-permute-start | bytes 3932168 | tf_op jit(solution)/shard_map/ppermute | solution.py:29
  166.1 5.1 %convolution_convert_fusion.1 = bf16[4,256,640]{2,1,0:T(8,128)(2,1)} fusion(bf16[4,256,640]{2,1,0:T(8,128)(2,1)} %bitcast.16, f32[4,256]{1,0:T(4,128)S(1)} %fusion.121, f32[4,256,256]{1,2,0:T(8,128)} %get-tuple-element.27), kind=kOutput, calls=%fused_computation.6 | convolution fusion | flops 336987392 | bytes 3674112 | tf_op jit(solution)/shard_map/cjt,cjd->ctd/dot_general | solution.py:116
  171.2 5.1 %convolution_convert_fusion = bf16[4,256,640]{2,1,0:T(8,128)(2,1)} fusion(bf16[4,256,640]{2,1,0:T(8,128)(2,1)} %collective-permute-done.3, f32[4,256]{1,0:T(4,128)S(1)} %fusion.121, f32[4,256,256]{1,2,0:T(8,128)} %get-tuple-element.27), kind=kOutput, calls=%fused_computation.5 | convolution fusion | flops 336987392 | bytes 3674112 | tf_op jit(solution)/shard_map/cjt,cjd->ctd/dot_general | solution.py:116
  176.2 4.3 %maximum_select_fusion = bf16[4,256,1280]{2,1,0:T(8,128)(2,1)} fusion(bf16[4,256,640]{2,1,0:T(8,128)(2,1)} %convolution_convert_fusion, bf16[4,256,640]{2,1,0:T(8,128)(2,1)} %convolution_convert_fusion.1, pred[]{:T(512)S(6)} %eq.4), kind=kLoop, calls=%fused_computation.1 | loop fusion | flops 11796480 | bytes 5242881 | tf_op jit(solution)/shard_map/jit(_where)/select_n | solution.py:119
  (74 shorter events, 31.9 us)
Async XLA Ops:
  0.0 119.3 %copy-start = (bf16[1280,1280]{1,0:T(8,128)(2,1)S(1)}, bf16[1280,1280]{1,0:T(8,128)(2,1)}, u32[]{:S(2)}) copy-start(bf16[1280,1280]{1,0:T(8,128)(2,1)} %param.10) | copy-start | bytes 9830404
  3.9 1.5 copy-start.2
  18.4 11.1 %collective-permute-start = (bf16[4,256,768]{1,0,2:T(4,128)(2,1)}, bf16[4,256,768]{1,0,2:T(4,128)(2,1)}, u32[]{:S(2)}, u32[]{:S(2)}) collective-permute-start(bf16[4,256,768]{1,0,2:T(4,128)(2,1)} %broadcast_dynamic-update-slice_fusion), channel_id=1, source_target_pairs={{0,1},{1,0},{2,3},{3,2},{4,5},{5,4},{6,7},{7,6},{8,9},{9,8},{10,11... | collective-permute-start | bytes 4718600 | tf_op jit(solution)/shard_map/ppermute | solution.py:29
  74.3 1.1 copy-start.4
  75.5 0.8 copy-start.1
  77.5 2.1 %copy-start.5 = (bf16[4,256,768]{2,1,0:T(8,128)(2,1)S(1)}, bf16[4,256,768]{2,1,0:T(8,128)(2,1)}, u32[]{:S(2)}) copy-start(bf16[4,256,768]{2,1,0:T(8,128)(2,1)} %copy-done.4) | copy-start | bytes 4718596
  112.0 0.7 copy-start.6
  112.8 5.7 %copy-start.8 = (bf16[1280]{0:T(1024)(128)(2,1)S(1)}, bf16[1280]{0:T(1024)(128)(2,1)}, u32[]{:S(2)}) copy-start(bf16[1280]{0:T(1024)(128)(2,1)} %param.9) | copy-start | bytes 7684
  114.0 1.2 copy-start.7
  115.4 3.8 %collective-permute-start.1 = (bf16[16,640]{1,0:T(8,128)(2,1)S(1)}, bf16[16,640]{1,0:T(8,128)(2,1)S(1)}, u32[]{:S(2)}, u32[]{:S(2)}) collective-permute-start(bf16[16,640]{1,0:T(8,128)(2,1)S(1)} %divide_convert_fusion.1), channel_id=1, source_target_pairs={{0,1},{1,0},{2,3},{3,2},{4,5},{5,4},{6,7},{7,6},{8,9},{9,8},{10,11... | collective-permute-start | bytes 61448 | tf_op jit(solution)/shard_map/ppermute | solution.py:29
  122.4 1.3 collective-permute-start.2
  161.2 4.5 %copy-start.3 = (f32[4,256,256]{1,2,0:T(8,128)S(1)}, f32[4,256,256]{1,2,0:T(8,128)}, u32[]{:S(2)}) copy-start(f32[4,256,256]{1,2,0:T(8,128)} %get-tuple-element.27) | copy-start | bytes 3145732
  162.4 8.8 %collective-permute-start.3 = (bf16[4,256,640]{2,1,0:T(8,128)(2,1)}, bf16[4,256,640]{2,1,0:T(8,128)(2,1)}, u32[]{:S(2)}, u32[]{:S(2)}) collective-permute-start(bf16[4,256,640]{2,1,0:T(8,128)(2,1)} %bitcast.16), channel_id=1, source_target_pairs={{0,1},{1,0},{2,3},{3,2},{4,5},{5,4},{6,7},{7,6},{8,9},{9,8},{10,11... | collective-permute-start | bytes 3932168 | tf_op jit(solution)/shard_map/ppermute | solution.py:29

commit v2 on v0

v2 whole, which is shorter than its diff:
```python
import jax
import jax.numpy as jnp
from jax import lax
from jax.experimental import pallas as pl
from jax.experimental.pallas import tpu as pltpu
from jax.sharding import PartitionSpec as P

BF16 = jnp.bfloat16
F32 = jnp.float32
CLIPS = 4
SLOTS = 256
TOK = 256
D = 1280
HALF = 640
STATS = CLIPS * HALF
ROW = STATS + 128
VMEM_LIMIT = 40 * 2**20


def coords(index):
    return index // 64, index // 16 % 4, index // 2 % 8, index % 2


def groups_by(key):
    found = {}
    for index in range(128):
        found.setdefault(key(*coords(index)), []).append(index)
    return list(found.values())


ALONG_X = groups_by(lambda y, x, z, core: (y, z, core))
ALONG_YZ = groups_by(lambda y, x, z, core: (x, core))


def exchange(value, groups):
    return lax.all_to_all(value, "seq", 0, 0, tiled=True, axis_index_groups=groups)


def swap_cores(value):
    return lax.ppermute(value, "seq", [(source, source ^ 1) for source in range(128)])


def params():
    return pltpu.CompilerParams(vmem_limit_bytes=VMEM_LIMIT)


def cost(flops, bytes_accessed):
    return pl.CostEstimate(flops=flops, bytes_accessed=bytes_accessed, transcendentals=0)


def stats_lanes(clip, peak, total):
    p1 = peak.astype(BF16).astype(F32)
    p2 = (peak - p1).astype(BF16).astype(F32)
    p3 = peak - p1 - p2
    t1 = total.astype(BF16).astype(F32)
    t2 = total - t1
    lane = lax.broadcasted_iota(jnp.int32, (peak.shape[0], 128), 1) - 8 * clip
    out = jnp.where(lane == 0, p1, 0.0)
    for k, column in enumerate((p2, p3, t1, t2)):
        out = jnp.where(lane == k + 1, column, out)
    return out


def read_stats(clip, stats):
    lane = lax.broadcasted_iota(jnp.int32, stats.shape, stats.ndim - 1) - 8 * clip
    peak = jnp.sum(jnp.where((lane >= 0) & (lane < 3), stats, 0.0), axis=-1, keepdims=True)
    total = jnp.sum(jnp.where((lane >= 3) & (lane < 5), stats, 0.0), axis=-1, keepdims=True)
    return peak, total


def keep_stats(clip, lanes, scratch):
    @pl.when(clip == 0)
    def _():
        scratch[...] = lanes

    @pl.when(clip > 0)
    def _():
        scratch[...] += lanes

    return scratch[...].astype(BF16)


def columns(clip):
    return pl.ds(pl.multiple_of(clip * HALF, 128), HALF)


def dispatch_kernel(core_ref, x_ref, phi_ref, send_ref, logits_ref, dispatch_ref, scratch):
    clip = pl.program_id(0)
    logits = jnp.dot(x_ref[0], phi_ref[...], preferred_element_type=F32)
    logits_ref[0] = logits
    turned = logits.T
    peak = jnp.max(turned, axis=1, keepdims=True)
    expo = jnp.exp(turned - peak)
    total = jnp.sum(expo, axis=1, keepdims=True)
    dispatch = expo.astype(BF16)
    dispatch_ref[0] = dispatch
    other = x_ref[0, :, columns(1 - core_ref[0])]
    send_ref[:, columns(clip)] = jnp.dot(dispatch, other, preferred_element_type=F32).astype(BF16)
    send_ref[:, STATS:] = keep_stats(clip, stats_lanes(clip, peak, total), scratch)


def dispatch_call(core, clips_x, slot_phi):
    return pl.pallas_call(
        dispatch_kernel,
        out_shape=(
            jax.ShapeDtypeStruct((SLOTS, ROW), BF16),
            jax.ShapeDtypeStruct((CLIPS, TOK, SLOTS), F32),
            jax.ShapeDtypeStruct((CLIPS, SLOTS, TOK), BF16),
        ),
        grid_spec=pltpu.PrefetchScalarGridSpec(
            num_scalar_prefetch=1,
            grid=(CLIPS,),
            in_specs=[
                pl.BlockSpec((1, TOK, D), lambda c, core: (c, 0, 0)),
                pl.BlockSpec((D, SLOTS), lambda c, core: (0, 0)),
            ],
            out_specs=(
                pl.BlockSpec((SLOTS, ROW), lambda c, core: (0, 0)),
                pl.BlockSpec((1, TOK, SLOTS), lambda c, core: (c, 0, 0)),
                pl.BlockSpec((1, SLOTS, TOK), lambda c, core: (c, 0, 0)),
            ),
            scratch_shapes=[pltpu.VMEM((SLOTS, 128), F32)],
        ),
        compiler_params=params(),
        cost_estimate=cost(2 * 1024 * 256 * 1920, 6 * 2**20),
        name="dispatch",
    )(core, clips_x, slot_phi)


def own_kernel(core_ref, x_ref, logits_ref, dispatch_ref, own_ref, comb_ref):
    own_ref[...] = jnp.dot(dispatch_ref[0], x_ref[0], preferred_element_type=F32)
    logits = logits_ref[0]
    weights = jnp.exp(logits - jnp.max(logits, axis=1, keepdims=True))
    comb_ref[0] = (weights / jnp.sum(weights, axis=1, keepdims=True)).astype(BF16)


def own_call(core, clips_x, logits, dispatch):
    return pl.pallas_call(
        own_kernel,
        out_shape=(
            jax.ShapeDtypeStruct((SLOTS, CLIPS * HALF), F32),
            jax.ShapeDtypeStruct((CLIPS, TOK, SLOTS), BF16),
        ),
        grid_spec=pltpu.PrefetchScalarGridSpec(
            num_scalar_prefetch=1,
            grid=(CLIPS,),
            in_specs=[
                pl.BlockSpec((1, TOK, HALF), lambda c, core: (c, 0, core[0])),
                pl.BlockSpec((1, TOK, SLOTS), lambda c, core: (c, 0, 0)),
                pl.BlockSpec((1, SLOTS, TOK), lambda c, core: (c, 0, 0)),
            ],
            out_specs=(
                pl.BlockSpec((SLOTS, HALF), lambda c, core: (0, c)),
                pl.BlockSpec((1, TOK, SLOTS), lambda c, core: (c, 0, 0)),
            ),
        ),
        compiler_params=params(),
        cost_estimate=cost(2 * 1024 * 256 * 640, 6 * 2**20),
        name="own_half",
    )(core, clips_x, logits, dispatch)


def merge_cores_kernel(own_ref, mine_ref, arrived_ref, theirs_ref, out_ref, scratch):
    clip = pl.program_id(0)
    peak_a, total_a = read_stats(clip, mine_ref[...].astype(F32))
    peak_b, total_b = read_stats(clip, theirs_ref[...].astype(F32))
    peak = jnp.maximum(peak_a, peak_b)
    fa = jnp.exp(peak_a - peak)
    fb = jnp.exp(peak_b - peak)
    value = (fa * own_ref[...] + fb * arrived_ref[...].astype(F32)).astype(BF16)
    stats = keep_stats(clip, stats_lanes(clip, peak, fa * total_a + fb * total_b), scratch)
    for y in range(2):
        for x in range(4):
            rows = slice((y * 4 + x) * 32, (y * 4 + x) * 32 + 32)
            out_ref[x, y * 32 : y * 32 + 32, columns(clip)] = value[rows]
            out_ref[x, y * 32 : y * 32 + 32, STATS:] = stats[rows]


def merge_cores_call(own, sent, arrived):
    return pl.pallas_call(
        merge_cores_kernel,
        out_shape=jax.ShapeDtypeStruct((4, 64, ROW), BF16),
        grid=(CLIPS,),
        in_specs=[
            pl.BlockSpec((SLOTS, HALF), lambda c: (0, c)),
            pl.BlockSpec((SLOTS, 128), lambda c: (0, STATS // 128)),
            pl.BlockSpec((SLOTS, HALF), lambda c: (0, c)),
            pl.BlockSpec((SLOTS, 128), lambda c: (0, STATS // 128)),
        ],
        out_specs=pl.BlockSpec((4, 64, ROW), lambda c: (0, 0, 0)),
        scratch_shapes=[pltpu.VMEM((SLOTS, 128), F32)],
        compiler_params=params(),
        cost_estimate=cost(2**20, 6 * 2**20),
        name="merge_cores",
    )(own, sent, arrived, arrived)


def merge(clip, sources, value_of, stats_of):
    stats = [read_stats(clip, stats_of(k)) for k in range(sources)]
    peak = stats[0][0]
    for p, _ in stats[1:]:
        peak = jnp.maximum(peak, p)
    value, total = None, None
    for k, (p, t) in enumerate(stats):
        factor = jnp.exp(p - peak)
        v = factor * value_of(k)
        value = v if k == 0 else value + v
        total = factor * t if k == 0 else total + factor * t
    return value, peak, total


def merge_x_kernel(value_ref, stats_ref, out_ref, scratch):
    clip = pl.program_id(0)
    value, peak, total = merge(
        clip, 4, lambda k: value_ref[k].astype(F32), lambda k: stats_ref[k].astype(F32)
    )
    value = value.astype(BF16)
    stats = keep_stats(clip, stats_lanes(clip, peak, total), scratch)
    for piece in range(16):
        rows = slice(piece * 4, piece * 4 + 4)
        out_ref[piece, :, columns(clip)] = value[rows]
        out_ref[piece, :, STATS:] = stats[rows]


def merge_x_call(arrived):
    return pl.pallas_call(
        merge_x_kernel,
        out_shape=jax.ShapeDtypeStruct((16, 4, ROW), BF16),
        grid=(CLIPS,),
        in_specs=[
            pl.BlockSpec((4, 64, HALF), lambda c: (0, 0, c)),
            pl.BlockSpec((4, 64, 128), lambda c: (0, 0, STATS // 128)),
        ],
        out_specs=pl.BlockSpec((16, 4, ROW), lambda c: (0, 0, 0)),
        scratch_shapes=[pltpu.VMEM((64, 128), F32)],
        compiler_params=params(),
        cost_estimate=cost(2**20, 2 * 2**20),
        name="merge_x",
    )(arrived, arrived)


def merge_yz_kernel(value_ref, out_ref):
    for clip in range(CLIPS):
        value, _, total = merge(
            clip,
            16,
            lambda k: value_ref[k, :, clip * HALF : clip * HALF + HALF].astype(F32),
            lambda k: value_ref[k, :, STATS:].astype(F32),
        )
        out_ref[clip] = (value / total).astype(BF16)


def merge_yz_call(arrived):
    return pl.pallas_call(
        merge_yz_kernel,
        out_shape=jax.ShapeDtypeStruct((CLIPS, 4, HALF), BF16),
        compiler_params=params(),
        cost_estimate=cost(2**20, 2**19),
        name="merge_yz",
    )(arrived)


def spread_kernel(value_ref, out_ref):
    for x in range(4):
        for piece in range(16):
            out_ref[x, piece * 4 : piece * 4 + 4, :] = value_ref[piece]


def spread_call(value):
    return pl.pallas_call(
        spread_kernel,
        out_shape=jax.ShapeDtypeStruct((4, 64, CLIPS * HALF), BF16),
        compiler_params=params(),
        cost_estimate=cost(2**18, 2 * 2**20),
        name="spread_x",
    )(value)


def mix_kernel(side_ref, comb_ref, slots_ref, *rest):
    out_ref = rest[-1]
    pieces = [slots_ref[x, y * 32 : y * 32 + 32, :] for y in range(2) for x in range(4)]
    slots = jnp.concatenate(pieces, axis=0)
    out_ref[0] = jnp.dot(comb_ref[0], slots, preferred_element_type=F32).astype(BF16)


def mix_call(side, comb, slots, base=None):
    more = [] if base is None else [base]
    return pl.pallas_call(
        mix_kernel,
        out_shape=jax.ShapeDtypeStruct((CLIPS, TOK, D), BF16),
        grid_spec=pltpu.PrefetchScalarGridSpec(
            num_scalar_prefetch=1,
            grid=(CLIPS,),
            in_specs=[
                pl.BlockSpec((1, TOK, SLOTS), lambda c, side: (c, 0, 0)),
                pl.BlockSpec((4, 64, HALF), lambda c, side: (0, 0, c)),
            ]
            + [pl.BlockSpec(memory_space=pl.ANY)] * len(more),
            out_specs=pl.BlockSpec((1, TOK, HALF), lambda c, side: (c, 0, side[0])),
        ),
        input_output_aliases={3: 0} if more else {},
        compiler_params=params(),
        cost_estimate=cost(2 * 1024 * 256 * 640, 4 * 2**20),
        name="mix",
    )(side, comb, slots, *more)


def per_device(clips_x, slot_phi, w_in, b_in, w_out, b_out):
    me = lax.axis_index("seq")
    core = (me % 2).astype(jnp.int32)
    mine = core * HALF
    core_ref = core[None]
    sent, logits, dispatch = dispatch_call(core_ref, clips_x, slot_phi)
    arrived = swap_cores(sent)
    own, comb = own_call(core_ref, clips_x, logits, dispatch)
    packed = merge_cores_call(own, sent, arrived)
    packed = exchange(packed, ALONG_X)
    packed = merge_x_call(packed)
    packed = exchange(packed, ALONG_YZ)
    slot_in = merge_yz_call(packed).reshape(CLIPS * 4, HALF)
    partner = swap_cores(slot_in)
    rows = jnp.where(
        core == 0,
        jnp.concatenate([slot_in, partner], axis=1),
        jnp.concatenate([partner, slot_in], axis=1),
    )
    pre = jnp.dot(rows, w_in, preferred_element_type=F32)
    hidden = jax.nn.gelu(pre + b_in.astype(F32), approximate=False).astype(BF16)
    partial = jnp.dot(hidden, w_out, preferred_element_type=F32)
    part_mine = jnp.where(core == 0, partial[:, :HALF], partial[:, HALF:])
    part_theirs = jnp.where(core == 0, partial[:, HALF:], partial[:, :HALF])
    bias = lax.dynamic_slice(b_out, (me // 2, mine), (1, HALF)).astype(F32)
    summed = part_mine + swap_cores(part_theirs.astype(BF16)).astype(F32)
    slot_out = (summed + bias).astype(BF16)
    slot_out = slot_out.reshape(CLIPS, 4, HALF).transpose(1, 0, 2).reshape(1, 4, CLIPS * HALF)
    gathered = exchange(jnp.broadcast_to(slot_out, (16, 4, CLIPS * HALF)), ALONG_YZ)
    gathered = exchange(spread_call(gathered), ALONG_X)
    other = swap_cores(gathered)
    mixed = mix_call(core_ref, comb, gathered)
    return mix_call(1 - core_ref, comb, other, mixed)


def solution(mesh):
    placed = (P("clip", "seq", None), P(), P(None, "seq"), P("seq"), P("seq", None), P())
    return jax.shard_map(
        per_device, mesh=mesh, in_specs=placed, out_specs=P("clip", "seq", None), check_vma=False
    )
```

time: 1760 us -> 110 us (0.06)
  waiting for transfers between devices: 1050 us -> 2.5 us
  blocking collectives: 658 us -> 75.4 us
    unnamed x3 -> x0, waiting for transfers between devices: 943 us -> none
    psum x1 -> x0, blocking collectives: 331 us -> none  [per_device(): col_total = lax.psum(jnp.sum(expo, axis=1), 'seq')]
    pmax x1 -> x0, blocking collectives: 328 us -> none  [per_device(): col_max = lax.pmax(local_max, 'seq')]
    all_gather x1 -> x0, waiting for transfers between devices: 106 us -> none  [per_device(): lax.all_gather(slot_out, 'seq', axis=0, tiled=True)]
    all_to_all x0 -> x4, blocking collectives: none -> 75.4 us  [exchange(): lax.all_to_all(value, 'seq', 0, 0, tiled=True, axis_index_groups=groups)]
  transfers between devices with their start and end apart: 4 -> 4, of which waited for: 4 -> 4; matrix products, arithmetic and copies ran while one was open for 0% -> 1% of each run, Pallas kernels for 0% -> 3%
where the time goes in v2:
time: 110 us
  blocking collectives  75.4 us (69%)
  Pallas kernels  14.1 us (13%)
  starting transfers between devices  10.5 us (10%)
  local copies, waits for them, and re-layouts  3.11 us (3%)
  matrix products  3.11 us (3%)
  waiting for transfers between devices  2.5 us (2%)
    all_to_all x4, blocking collectives, exchange(): lax.all_to_all(value, 'seq', 0, 0, tiled=True, axis_index_groups=groups)  75.4 us
    ppermute x4, starting transfers between devices, swap_cores(): lax.ppermute(value, 'seq', [(source, source ^ 1) for source in range(128)])  10.5 us
    pallas_call x2, Pallas kernels, mix_call(): pl.pallas_call(mix_kernel, out_shape=jax.ShapeDtypeStruct((CLIPS, TOK, D)...  4.75 us
    pallas_call x1, Pallas kernels, dispatch_call(): pl.pallas_call(dispatch_kernel, out_shape=(jax.ShapeDtypeStruct((SLOTS, R...  3.9 us
    dot_general x1, matrix products, per_device(): partial = jnp.dot(hidden, w_out, preferred_element_type=F32)  3.11 us
    unnamed x12, local copies, waits for them, and re-layouts  3 us
    ppermute x4, waiting for transfers between devices, swap_cores(): lax.ppermute(value, 'seq', [(source, source ^ 1) for source in range(128)])  2.5 us
  transfers between devices with their start and end apart: 4, of which 4 were waited for; matrix products, arithmetic and copies ran while one was open for 1% of the time, Pallas kernels for 3%

profile of v2, /device:TPU:1, one launch (start us, length us, event | category | flops | bytes accessed | tf_op | source)
XLA Modules:
  0.0 109.6 jit_solution(10634917978817829541)
XLA Ops:
  0.0 1.9 %copy-done.1 = bf16[4,256,1280]{2,1,0:T(8,128)(2,1)S(1)} copy-done((bf16[4,256,1280]{2,1,0:T(8,128)(2,1)S(1)}, bf16[4,256,1280]{2,1,0:T(8,128)(2,1)}, u32[]{:S(2)}) %copy-start.1) | copy-done | bytes 2621464
  1.9 1.1 copy-done.4
  3.0 3.9 %dispatch.1 = (bf16[256,2688]{1,0:T(8,128)(2,1)S(1)}, f32[4,256,256]{2,1,0:T(8,128)S(1)}, bf16[4,256,256]{2,1,0:T(8,128)(2,1)S(1)}) custom-call(s32[1]{0:T(128)} %bitcast.core_ref.side_ref, bf16[4,256,1280]{2,1,0:T(8,128)(2,1)S(1)} %copy-done.1, bf16[1280,256]{1,0:T(8,128)(2,1)S(1)} %copy-done.4), custom_call_target="tpu_custom_call" | custom-call | flops 1006632960 | bytes 6291456 | tf_op jit(solution)/shard_map/dispatch/pallas_call | solution.py:103
  6.9 3.3 %collective-permute-start = (bf16[256,2688]{1,0:T(8,128)(2,1)S(1)}, bf16[256,2688]{1,0:T(8,128)(2,1)S(1)}, u32[]{:S(2)}, u32[]{:S(2)}) collective-permute-start(bf16[256,2688]{1,0:T(8,128)(2,1)S(1)} %get-tuple-element.14.mine_ref), channel_id=1, source_target_pairs={{0,1},{1,0},{2,3},{3,2},{4,5},{5,4},{6,7},{7,6},{8,9},{9,8},{10,11... | collective-permute-start | bytes 4128776 | tf_op jit(solution)/shard_map/ppermute | solution.py:40
  10.2 1.4 %own_half.1 = (f32[256,2560]{1,0:T(8,128)S(1)}, bf16[4,256,256]{2,1,0:T(8,128)(2,1)S(1)}) custom-call(s32[1]{0:T(128)} %bitcast.core_ref.side_ref, bf16[4,256,1280]{2,1,0:T(8,128)(2,1)S(1)} %copy-done.1, f32[4,256,256]{2,1,0:T(8,128)S(1)} %get-tuple-element.10.logits_ref, bf16[4,256,256]{2,1,0:T(8,128)(2,1)S(1)} %get-tuple-element.11.dispatch_ref), custom_call_target="tpu_custom_call" | custom-call | flops 335544320 | bytes 6291456 | tf_op jit(solution)/shard_map/own_half/pallas_call | solution.py:138
  11.7 1.3 %collective-permute-done.arrived_ref.theirs_ref = bf16[256,2688]{1,0:T(8,128)(2,1)S(1)} collective-permute-done((bf16[256,2688]{1,0:T(8,128)(2,1)S(1)}, bf16[256,2688]{1,0:T(8,128)(2,1)S(1)}, u32[]{:S(2)}, u32[]{:S(2)}) %collective-permute-start) | collective-permute-done | bytes 1376288 | tf_op jit(solution)/shard_map/ppermute | solution.py:40
  13.0 2.1 %merge_cores.1 = bf16[4,64,2688]{2,1,0:T(8,128)(2,1)S(1)} custom-call(f32[256,2560]{1,0:T(8,128)S(1)} %get-tuple-element.13.own_ref, bf16[256,2688]{1,0:T(8,128)(2,1)S(1)} %get-tuple-element.14.mine_ref, bf16[256,2688]{1,0:T(8,128)(2,1)S(1)} %collective-permute-done.arrived_ref.theirs_ref, bf16[256,2688]{1,0:T(8,128)(2,1)S(1)} %collective-permute-done.arrived_ref.theirs_ref), custom_call_target="tpu_custom_call" | custom-call | flops 1048576 | bytes 6291456 | tf_op jit(solution)/shard_map/merge_cores/pallas_call | solution.py:180
  15.1 20.5 %all_to_all.20.value_ref.stats_ref = bf16[4,64,2688]{2,1,0:T(8,128)(2,1)S(1)} all-to-all(bf16[4,64,2688]{2,1,0:T(8,128)(2,1)S(1)} %merge_cores.1), channel_id=1, replica_groups={{0,16,32,48},{1,17,33,49},{2,18,34,50},{3,19,35,51},{4,20,36,52},{5,21,..., dimensions={0} | all-to-all | bytes 2752512 | tf_op jit(solution)/shard_map/all_to_all | solution.py:36
  35.6 1.3 %merge_x.1 = bf16[16,4,2688]{2,1,0:T(4,128)(2,1)S(1)} custom-call(bf16[4,64,2688]{2,1,0:T(8,128)(2,1)S(1)} %all_to_all.20.value_ref.stats_ref, bf16[4,64,2688]{2,1,0:T(8,128)(2,1)S(1)} %all_to_all.20.value_ref.stats_ref), custom_call_target="tpu_custom_call" | custom-call | flops 1048576 | bytes 2097152 | tf_op jit(solution)/shard_map/merge_x/pallas_call | solution.py:226
  36.9 21.0 %all_to_all.21.value_ref = bf16[16,4,2688]{2,1,0:T(4,128)(2,1)S(1)} all-to-all(bf16[16,4,2688]{2,1,0:T(4,128)(2,1)S(1)} %merge_x.1), channel_id=1, replica_groups={{0,2,4,6,8,10,12,14,64,66,68,70,72,74,76,78},{1,3,5,7,9,11,13,15,65,67,..., dimensions={0} | all-to-all | bytes 688128 | tf_op jit(solution)/shard_map/all_to_all | solution.py:36
  57.9 0.3 merge_yz.1
  58.2 3.4 %collective-permute-start.1 = (bf16[16,640]{1,0:T(8,128)(2,1)S(1)}, bf16[16,640]{1,0:T(8,128)(2,1)S(1)}, u32[]{:S(2)}, u32[]{:S(2)}) collective-permute-start(bf16[16,640]{1,0:T(8,128)(2,1)S(1)} %reshape.9), channel_id=1, source_target_pairs={{0,1},{1,0},{2,3},{3,2},{4,5},{5,4},{6,7},{7,6},{8,9},{9,8},{10,11... | collective-permute-start | bytes 61448 | tf_op jit(solution)/shard_map/ppermute | solution.py:40
  61.6 0.8 collective-permute-done.1
  62.4 3.1 %fusion.10 = f32[16,1280]{1,0:T(8,128)S(1)} fusion(bf16[1280,1280]{1,0:T(8,128)(2,1)S(1)} %copy-done, bf16[1280,1280]{1,0:T(8,128)(2,1)} %param.8, bf16[16,640]{1,0:T(8,128)(2,1)S(1)} %collective-permute-done.1, bf16[16,640]{1,0:T(8,128)(2,1)S(1)} %reshape.9, f32[1280]{0:T(1024)S(1)} %convert_element_type.16, pred[]{:T(512)S(6)} %eq.4), kind=kOutput, calls=%fused_computation.20 | convolution fusion | flops 106393600 | bytes 6681601 | tf_op jit(solution)/shard_map/dot_general | solution.py:329
  65.6 0.4 collective-permute-start.2
  66.0 0.8 convert_reduce_fusion
  66.9 0.1 broadcast_in_dim.13
  67.0 15.9 %all_to_all.22.value_ref = bf16[16,4,2560]{2,1,0:T(4,128)(2,1)S(1)} all-to-all(bf16[16,4,2560]{2,1,0:T(4,128)(2,1)S(1)} %broadcast_in_dim.13), channel_id=1, replica_groups={{0,2,4,6,8,10,12,14,64,66,68,70,72,74,76,78},{1,3,5,7,9,11,13,15,65,67,..., dimensions={0} | all-to-all | bytes 655360 | tf_op jit(solution)/shard_map/all_to_all | solution.py:36
  82.9 0.3 spread_x.1
  83.3 18.0 %all_to_all.23.slots_ref = bf16[4,64,2560]{2,1,0:T(8,128)(2,1)S(1)} all-to-all(bf16[4,64,2560]{2,1,0:T(8,128)(2,1)S(1)} %spread_x.1), channel_id=1, replica_groups={{0,16,32,48},{1,17,33,49},{2,18,34,50},{3,19,35,51},{4,20,36,52},{5,21,..., dimensions={0} | all-to-all | bytes 2621440 | tf_op jit(solution)/shard_map/all_to_all | solution.py:36
  101.2 3.3 %collective-permute-start.3 = (bf16[4,64,2560]{2,1,0:T(8,128)(2,1)S(1)}, bf16[4,64,2560]{2,1,0:T(8,128)(2,1)S(1)}, u32[]{:S(2)}, u32[]{:S(2)}) collective-permute-start(bf16[4,64,2560]{2,1,0:T(8,128)(2,1)S(1)} %all_to_all.23.slots_ref), channel_id=1, source_target_pairs={{0,1},{1,0},{2,3},{3,2},{4,5},{5,4},{6,7},{7,6},{8,9},{9,8},{10,11... | collective-permute-start | bytes 3932168 | tf_op jit(solution)/shard_map/ppermute | solution.py:40
  104.6 2.4 %mix.2.rest_0_ = bf16[4,256,1280]{2,1,0:T(8,128)(2,1)} custom-call(s32[1]{0:T(128)} %bitcast.core_ref.side_ref, bf16[4,256,256]{2,1,0:T(8,128)(2,1)S(1)} %copy-done.3, bf16[4,64,2560]{2,1,0:T(8,128)(2,1)S(1)} %all_to_all.23.slots_ref), custom_call_target="tpu_custom_call" | custom-call | flops 335544320 | bytes 4194304 | tf_op jit(solution)/shard_map/mix/pallas_call | solution.py:288
  106.9 0.3 collective-permute-done.3.slots_ref
  107.2 2.4 %mix.3 = bf16[4,256,1280]{2,1,0:T(8,128)(2,1)} custom-call(s32[1]{0:T(128)S(6)} %sub.7.side_ref, bf16[4,256,256]{2,1,0:T(8,128)(2,1)S(1)} %copy-done.3, bf16[4,64,2560]{2,1,0:T(8,128)(2,1)S(1)} %collective-permute-done.3.slots_ref, bf16[4,256,1280]{2,1,0:T(8,128)(2,1)} %mix.2.rest_0_), custom_call_target="tpu_custom_call", output_to_operand_aliasing={{}: (3, {})} | custom-call | flops 335544320 | bytes 4194304 | tf_op jit(solution)/shard_map/mix/pallas_call | solution.py:288
  (16 shorter events, 0.1 us)
Async XLA Ops:
  0.0 62.4 %copy-start = (bf16[1280,1280]{1,0:T(8,128)(2,1)S(1)}, bf16[1280,1280]{1,0:T(8,128)(2,1)}, u32[]{:S(2)}) copy-start(bf16[1280,1280]{1,0:T(8,128)(2,1)} %param.10) | copy-start | bytes 9830404
  0.0 1.9 %copy-start.1 = (bf16[4,256,1280]{2,1,0:T(8,128)(2,1)S(1)}, bf16[4,256,1280]{2,1,0:T(8,128)(2,1)}, u32[]{:S(2)}) copy-start(bf16[4,256,1280]{2,1,0:T(8,128)(2,1)} %x_ref.3) | copy-start | bytes 7864324
  1.9 1.1 copy-start.4
  6.9 6.1 %collective-permute-start = (bf16[256,2688]{1,0:T(8,128)(2,1)S(1)}, bf16[256,2688]{1,0:T(8,128)(2,1)S(1)}, u32[]{:S(2)}, u32[]{:S(2)}) collective-permute-start(bf16[256,2688]{1,0:T(8,128)(2,1)S(1)} %get-tuple-element.14.mine_ref), channel_id=1, source_target_pairs={{0,1},{1,0},{2,3},{3,2},{4,5},{5,4},{6,7},{7,6},{8,9},{9,8},{10,11... | collective-permute-start | bytes 4128776 | tf_op jit(solution)/shard_map/ppermute | solution.py:40
  11.6 3.5 %copy-start.2 = (bf16[4,256,256]{2,1,0:T(8,128)(2,1)}, bf16[4,256,256]{2,1,0:T(8,128)(2,1)S(1)}, u32[]{:S(2)}) copy-start(bf16[4,256,256]{2,1,0:T(8,128)(2,1)S(1)} %get-tuple-element.12.comb_ref) | copy-start | bytes 1572868
  35.6 26.0 %copy-start.5 = (bf16[1280]{0:T(1024)(128)(2,1)S(1)}, bf16[1280]{0:T(1024)(128)(2,1)}, u32[]{:S(2)}) copy-start(bf16[1280]{0:T(1024)(128)(2,1)} %param.9) | copy-start | bytes 7684
  58.2 4.3 %collective-permute-start.1 = (bf16[16,640]{1,0:T(8,128)(2,1)S(1)}, bf16[16,640]{1,0:T(8,128)(2,1)S(1)}, u32[]{:S(2)}, u32[]{:S(2)}) collective-permute-start(bf16[16,640]{1,0:T(8,128)(2,1)S(1)} %reshape.9), channel_id=1, source_target_pairs={{0,1},{1,0},{2,3},{3,2},{4,5},{5,4},{6,7},{7,6},{8,9},{9,8},{10,11... | collective-permute-start | bytes 61448 | tf_op jit(solution)/shard_map/ppermute | solution.py:40
  65.6 1.3 %collective-permute-start.2 = (bf16[16,640]{1,0:T(8,128)(2,1)S(1)}, bf16[16,640]{1,0:T(8,128)(2,1)S(1)}, u32[]{:S(2)}, u32[]{:S(2)}) collective-permute-start(bf16[16,640]{1,0:T(8,128)(2,1)S(1)} %select_convert_fusion), channel_id=1, source_target_pairs={{0,1},{1,0},{2,3},{3,2},{4,5},{5,4},{6,7},{7,6},{8,9},{9,8},{10,11... | collective-permute-start | bytes 61448 | tf_op jit(solution)/shard_map/ppermute | solution.py:40
  66.9 37.7 %copy-start.3 = (bf16[4,256,256]{2,1,0:T(8,128)(2,1)S(1)}, bf16[4,256,256]{2,1,0:T(8,128)(2,1)}, u32[]{:S(2)}) copy-start(bf16[4,256,256]{2,1,0:T(8,128)(2,1)} %copy-done.2) | copy-start | bytes 1572868
  101.2 6.0 %collective-permute-start.3 = (bf16[4,64,2560]{2,1,0:T(8,128)(2,1)S(1)}, bf16[4,64,2560]{2,1,0:T(8,128)(2,1)S(1)}, u32[]{:S(2)}, u32[]{:S(2)}) collective-permute-start(bf16[4,64,2560]{2,1,0:T(8,128)(2,1)S(1)} %all_to_all.23.slots_ref), channel_id=1, source_target_pairs={{0,1},{1,0},{2,3},{3,2},{4,5},{5,4},{6,7},{7,6},{8,9},{9,8},{10,11... | collective-permute-start | bytes 3932168 | tf_op jit(solution)/shard_map/ppermute | solution.py:40

commit v3 on v0

v3 whole, which is shorter than its diff:
```python
import functools

import jax
import jax.numpy as jnp
from jax import lax
from jax.experimental import pallas as pl
from jax.experimental.pallas import tpu as pltpu
from jax.sharding import PartitionSpec as P

BF16 = jnp.bfloat16
F32 = jnp.float32
CLIPS = 4
SLOTS = 256
TOK = 256
D = 1280
HALF = 640
STATS = CLIPS * HALF
ROW = STATS + 128
VMEM_LIMIT = 8 * 2**20
DISPATCH_VMEM = 49 * 2**20


def coords(index):
    return index // 64, index // 16 % 4, index // 2 % 8, index % 2


def groups_by(key):
    found = {}
    for index in range(128):
        found.setdefault(key(*coords(index)), []).append(index)
    return list(found.values())


STAGE_TWO = groups_by(lambda y, x, z, core: (core, x) if core == 0 else (core, y, z % 2))


def peer(index, k):
    y, x, z, core = coords(index)
    if core == 0:
        x = (x + (0, 1, 3, 2)[k]) % 4
    else:
        y, z = y ^ (k // 2), z ^ (k % 2)
    return ((y * 4 + x) * 8 + z) * 2 + core


def exchange(value, groups):
    return lax.all_to_all(value, "seq", 0, 0, tiled=True, axis_index_groups=groups)


def swap_cores(value):
    return lax.ppermute(value, "seq", [(source, source ^ 1) for source in range(128)])


def send_piece(value, k):
    return lax.ppermute(value, "seq", [(source, peer(source, k)) for source in range(128)])


def params(limit=VMEM_LIMIT):
    return pltpu.CompilerParams(vmem_limit_bytes=limit)


def cost(flops, bytes_accessed):
    return pl.CostEstimate(flops=flops, bytes_accessed=bytes_accessed, transcendentals=0)


DISPATCH_COST = cost(2 * 1024 * 256 * 1920, 6 * 2**20)


def stats_lanes(clip, peak, total):
    p1 = peak.astype(BF16).astype(F32)
    p2 = (peak - p1).astype(BF16).astype(F32)
    p3 = peak - p1 - p2
    t1 = total.astype(BF16).astype(F32)
    t2 = total - t1
    lane = lax.broadcasted_iota(jnp.int32, (peak.shape[0], 128), 1) - 8 * clip
    out = jnp.where(lane == 0, p1, 0.0)
    for k, column in enumerate((p2, p3, t1, t2)):
        out = jnp.where(lane == k + 1, column, out)
    return out


def read_stats(clip, stats):
    lane = lax.broadcasted_iota(jnp.int32, stats.shape, stats.ndim - 1) - 8 * clip
    peak = jnp.sum(jnp.where((lane >= 0) & (lane < 3), stats, 0.0), axis=-1, keepdims=True)
    total = jnp.sum(jnp.where((lane >= 3) & (lane < 5), stats, 0.0), axis=-1, keepdims=True)
    return peak, total


def column_slice(clip):
    return slice(clip * HALF, clip * HALF + HALF)


def dynamic_half(core):
    return pl.ds(pl.multiple_of(core * HALF, 128), HALF)


def phi_rows(core):
    return pl.ds(pl.multiple_of(core * HALF, 128), HALF)


def order_matrix(core, where_ref, start):
    row = lax.broadcasted_iota(jnp.int32, (SLOTS, 1), 0)
    k, rest = row >> 6, row & 63
    piece = jnp.where(
        k < 2,
        jnp.where(k == 0, where_ref[start], where_ref[start + 1]),
        jnp.where(k == 2, where_ref[start + 2], where_ref[start + 3]),
    )
    by_x = ((rest >> 5) << 7) | (piece << 5) | (rest & 31)
    by_yz = ((piece >> 1) << 7) | ((rest >> 4) << 5) | (((rest >> 2) & 3) << 3) | ((piece & 1) << 2) | (rest & 3)
    slot = jnp.where(core == 0, by_x, by_yz)
    return jnp.where(lax.broadcasted_iota(jnp.int32, (SLOTS, SLOTS), 1) == slot, 1.0, 0.0).astype(BF16)


VMEM_SPEC = pl.BlockSpec(memory_space=pltpu.VMEM)
SMEM_SPEC = pl.BlockSpec(memory_space=pltpu.SMEM)
HBM_SPEC = pl.BlockSpec(memory_space=pltpu.HBM)
SENT, OTHER_SENT, GOT, OTHER_GOT = 1, 5, 9, 13
SEND_ORDER = (3, 1, 2, 0)


def dispatch_kernel(where_ref, x_hbm, phi_hbm, *refs):
    send_refs, (logits_ref, dispatch_ref, x_ref, other_ref, phi_ref, x_sem, phi_sem) = refs[:4], refs[4:]
    core = where_ref[0]
    phi_copy = pltpu.make_async_copy(phi_hbm, phi_ref, phi_sem)
    phi_copy.start()
    copies = []
    for clip in range(CLIPS):
        for side, target in ((core, x_ref), (1 - core, other_ref)):
            source = x_hbm.at[clip, :, dynamic_half(side)]
            copies.append(pltpu.make_async_copy(source, target.at[clip], x_sem.at[len(copies)]))
            copies[-1].start()
    order = order_matrix(1 - core, where_ref, OTHER_SENT)
    phi_copy.wait()
    phi = jnp.concatenate([phi_ref[phi_rows(core), :], phi_ref[phi_rows(1 - core), :]], axis=0)
    for copy in copies:
        copy.wait()
    tokens = jnp.concatenate(
        [x_ref[...].reshape(CLIPS * TOK, HALF), other_ref[...].reshape(CLIPS * TOK, HALF)], axis=1
    )
    all_logits = jnp.dot(tokens, phi, preferred_element_type=F32)
    stats = jnp.zeros((SLOTS, 128), F32)
    for clip in range(CLIPS):
        logits = all_logits[clip * TOK : clip * TOK + TOK]
        logits_ref[clip] = logits
        peak = jnp.max(logits, axis=0, keepdims=True)
        expo = jnp.exp(logits - peak)
        total = jnp.sum(expo, axis=0, keepdims=True)
        dispatch = lax.dot_general(
            order, expo.astype(BF16), (((1,), (1,)), ((), ())), preferred_element_type=F32
        ).astype(BF16)
        dispatch_ref[clip] = dispatch
        sums = jnp.dot(dispatch, other_ref[clip], preferred_element_type=F32).astype(BF16)
        for k in range(4):
            send_refs[k][:, column_slice(clip)] = sums[k * 64 : k * 64 + 64]
        both = jnp.concatenate([peak, total, jnp.zeros((6, SLOTS), F32)], axis=0).T
        stats += stats_lanes(clip, both[:, 0:1], both[:, 1:2])
    stats = jnp.dot(order, stats.astype(BF16), preferred_element_type=F32).astype(BF16)
    for k in range(4):
        send_refs[k][:, STATS:] = stats[k * 64 : k * 64 + 64]


def dispatch_call(where, clips_x, slot_phi):
    return pl.pallas_call(
        dispatch_kernel,
        out_shape=tuple(jax.ShapeDtypeStruct((64, ROW), BF16) for _ in range(4))
        + (
            jax.ShapeDtypeStruct((CLIPS, TOK, SLOTS), F32),
            jax.ShapeDtypeStruct((CLIPS, SLOTS, TOK), BF16),
            jax.ShapeDtypeStruct((CLIPS, TOK, HALF), BF16),
        ),
        in_specs=[SMEM_SPEC, HBM_SPEC, HBM_SPEC],
        out_specs=(VMEM_SPEC,) * 7,
        scratch_shapes=[
            pltpu.VMEM((CLIPS, TOK, HALF), BF16),
            pltpu.VMEM((D, SLOTS), BF16),
            pltpu.SemaphoreType.DMA((2 * CLIPS,)),
            pltpu.SemaphoreType.DMA,
        ],
        compiler_params=params(DISPATCH_VMEM),
        cost_estimate=DISPATCH_COST,
        name="dispatch",
    )(where, clips_x, slot_phi)


def own_kernel(where_ref, x_ref, dispatch_ref, s0, s1, s2, s3, own_ref, stats_ref):
    core = where_ref[0]
    given = order_matrix(1 - core, where_ref, OTHER_SENT)
    order = order_matrix(core, where_ref, SENT)
    order = lax.dot_general(order, given, (((1,), (1,)), ((), ())), preferred_element_type=F32).astype(BF16)
    stats = jnp.concatenate([s[:, STATS:] for s in (s0, s1, s2, s3)], axis=0)
    stats_ref[...] = jnp.dot(order, stats, preferred_element_type=F32).astype(BF16)
    for clip in range(CLIPS):
        dispatch = jnp.dot(order, dispatch_ref[clip], preferred_element_type=F32).astype(BF16)
        own_ref[:, column_slice(clip)] = jnp.dot(dispatch, x_ref[clip], preferred_element_type=F32)


def own_call(where, x_half, dispatch, sent):
    return pl.pallas_call(
        own_kernel,
        out_shape=(
            jax.ShapeDtypeStruct((SLOTS, CLIPS * HALF), F32),
            jax.ShapeDtypeStruct((SLOTS, 128), BF16),
        ),
        in_specs=[SMEM_SPEC] + [VMEM_SPEC] * 6,
        out_specs=(VMEM_SPEC,) * 2,
        compiler_params=params(),
        cost_estimate=cost(2 * 1024 * 256 * 640, 6 * 2**20),
        name="own_half",
    )(where, x_half, dispatch, *sent)


def comb_kernel(where_ref, logits_ref, piece_ref, comb_ref, other_comb_ref, same_ref):
    core = where_ref[0]
    same_ref[...] = piece_ref[...]
    orders = order_matrix(core, where_ref, GOT), order_matrix(1 - core, where_ref, OTHER_GOT)
    for clip in range(CLIPS):
        logits = logits_ref[clip]
        weights = jnp.exp(logits - jnp.max(logits, axis=1, keepdims=True))
        comb = (weights / jnp.sum(weights, axis=1, keepdims=True)).astype(BF16)
        for order, out_ref in zip(orders, (comb_ref, other_comb_ref)):
            turned = lax.dot_general(comb, order, (((1,), (1,)), ((), ())), preferred_element_type=F32)
            out_ref[clip] = turned.astype(BF16)


def comb_call(where, logits, piece):
    return pl.pallas_call(
        comb_kernel,
        out_shape=(
            jax.ShapeDtypeStruct((CLIPS, TOK, SLOTS), BF16),
            jax.ShapeDtypeStruct((CLIPS, TOK, SLOTS), BF16),
            jax.ShapeDtypeStruct((64, CLIPS * HALF), BF16),
        ),
        in_specs=[SMEM_SPEC] + [VMEM_SPEC] * 2,
        out_specs=(VMEM_SPEC,) * 3,
        compiler_params=params(),
        cost_estimate=cost(2**27, 4 * 2**20),
        name="comb",
    )(where, logits, piece)


def merge_cores_kernel(k, own_ref, mine_ref, arrived_ref, out_ref):
    rows = slice(k * 64, k * 64 + 64)
    mine = mine_ref[rows].astype(F32)
    theirs = arrived_ref[:, STATS:].astype(F32)
    stats = jnp.zeros(mine.shape, F32)
    for clip in range(CLIPS):
        peak_a, total_a = read_stats(clip, mine)
        peak_b, total_b = read_stats(clip, theirs)
        peak = jnp.maximum(peak_a, peak_b)
        fa = jnp.exp(peak_a - peak)
        fb = jnp.exp(peak_b - peak)
        at = column_slice(clip)
        out_ref[:, at] = (fa * own_ref[rows, at] + fb * arrived_ref[:, at].astype(F32)).astype(BF16)
        stats += stats_lanes(clip, peak, fa * total_a + fb * total_b)
    out_ref[:, STATS:] = stats.astype(BF16)


def merge_cores_call(k, own, mine, arrived):
    return pl.pallas_call(
        functools.partial(merge_cores_kernel, k),
        out_shape=jax.ShapeDtypeStruct((64, ROW), BF16),
        in_specs=[VMEM_SPEC] * 3,
        out_specs=VMEM_SPEC,
        compiler_params=params(),
        cost_estimate=cost(2**20, 2**20),
        name="merge_cores",
    )(own, mine, arrived)


def merge(clip, sources, value_of, stats_of):
    stats = [read_stats(clip, stats_of(k)) for k in range(sources)]
    peak = stats[0][0]
    for p, _ in stats[1:]:
        peak = jnp.maximum(peak, p)
    value, total = None, None
    for k, (p, t) in enumerate(stats):
        factor = jnp.exp(p - peak)
        v = factor * value_of(k)
        value = v if k == 0 else value + v
        total = factor * t if k == 0 else total + factor * t
    return value, peak, total


def merge_four_kernel(*refs):
    piece_refs, out_ref = refs[:4], refs[4]
    all_stats = jnp.zeros((64, 128), F32)
    for clip in range(CLIPS):
        at = column_slice(clip)
        value, peak, total = merge(
            clip,
            4,
            lambda k: piece_refs[k][:, at].astype(F32),
            lambda k: piece_refs[k][:, STATS:].astype(F32),
        )
        value = value.astype(BF16)
        all_stats += stats_lanes(clip, peak, total)
        for piece in range(16):
            out_ref[piece, :, at] = value[piece * 4 : piece * 4 + 4]
    all_stats = all_stats.astype(BF16)
    for piece in range(16):
        out_ref[piece, :, STATS:] = all_stats[piece * 4 : piece * 4 + 4]


def merge_four_call(pieces):
    return pl.pallas_call(
        merge_four_kernel,
        out_shape=jax.ShapeDtypeStruct((16, 4, ROW), BF16),
        in_specs=[VMEM_SPEC] * 4,
        out_specs=VMEM_SPEC,
        compiler_params=params(),
        cost_estimate=cost(2**20, 2 * 2**20),
        name="merge_four",
    )(*pieces)


def merge_yz_kernel(value_ref, out_ref):
    for clip in range(CLIPS):
        value, _, total = merge(
            clip,
            16,
            lambda k: value_ref[k, :, clip * HALF : clip * HALF + HALF].astype(F32),
            lambda k: value_ref[k, :, STATS:].astype(F32),
        )
        out_ref[clip] = (value / total).astype(BF16)


def merge_yz_call(arrived):
    return pl.pallas_call(
        merge_yz_kernel,
        out_shape=jax.ShapeDtypeStruct((CLIPS, 4, HALF), BF16),
        in_specs=[VMEM_SPEC],
        out_specs=VMEM_SPEC,
        compiler_params=params(),
        cost_estimate=cost(2**20, 2**19),
        name="merge_yz",
    )(arrived)


def flatten_kernel(value_ref, out_ref):
    for piece in range(16):
        out_ref[piece * 4 : piece * 4 + 4, :] = value_ref[piece]


def flatten_call(value):
    return pl.pallas_call(
        flatten_kernel,
        out_shape=jax.ShapeDtypeStruct((64, CLIPS * HALF), BF16),
        in_specs=[VMEM_SPEC],
        out_specs=VMEM_SPEC,
        compiler_params=params(),
        cost_estimate=cost(2**18, 2**20),
        name="flatten",
    )(value)


def mixed_half(clip, comb_ref, pieces):
    slots = jnp.concatenate([piece[:, column_slice(clip)] for piece in pieces], axis=0)
    return jnp.dot(comb_ref[clip], slots, preferred_element_type=F32).astype(BF16)


def mix_own_kernel(comb_ref, p0, p1, p2, p3, out_ref):
    for clip in range(CLIPS):
        out_ref[clip] = mixed_half(clip, comb_ref, (p0, p1, p2, p3))


def mix_own_call(comb, pieces):
    return pl.pallas_call(
        mix_own_kernel,
        out_shape=jax.ShapeDtypeStruct((CLIPS, TOK, HALF), BF16),
        in_specs=[VMEM_SPEC] * 5,
        out_specs=VMEM_SPEC,
        compiler_params=params(),
        cost_estimate=cost(2 * 1024 * 256 * 640, 4 * 2**20),
        name="mix_own",
    )(comb, *pieces)


def mix_all_kernel(where_ref, own_ref, comb_ref, p0, p1, p2, p3, out_hbm, half_ref, own_sem, sem):
    core = where_ref[0]
    copies = [
        pltpu.make_async_copy(own_ref.at[c], out_hbm.at[c, :, dynamic_half(core)], own_sem.at[c]) for c in range(CLIPS)
    ]
    for copy in copies:
        copy.start()
    for clip in range(CLIPS):
        half_ref[clip] = mixed_half(clip, comb_ref, (p0, p1, p2, p3))
        target = out_hbm.at[clip, :, dynamic_half(1 - core)]
        copies.append(pltpu.make_async_copy(half_ref.at[clip], target, sem.at[clip]))
        copies[-1].start()
    for copy in copies:
        copy.wait()


def mix_all_call(where, own, comb, pieces):
    return pl.pallas_call(
        mix_all_kernel,
        out_shape=jax.ShapeDtypeStruct((CLIPS, TOK, D), BF16),
        in_specs=[SMEM_SPEC] + [VMEM_SPEC] * 6,
        out_specs=HBM_SPEC,
        scratch_shapes=[
            pltpu.VMEM((CLIPS, TOK, HALF), BF16),
            pltpu.SemaphoreType.DMA((CLIPS,)),
            pltpu.SemaphoreType.DMA((CLIPS,)),
        ],
        compiler_params=params(),
        cost_estimate=cost(2 * 1024 * 256 * 640, 6 * 2**20),
        name="mix_all",
    )(where, own, comb, *pieces)


def targets(core, y, x, z):
    group = y * 2 + z % 2
    sent = [jnp.where(core == 0, (x + (0, 1, 3, 2)[k]) % 4, group ^ k) for k in range(4)]
    got = [jnp.where(core == 0, (x + (0, 3, 1, 2)[k]) % 4, group ^ k) for k in range(4)]
    return sent, got


def per_device(clips_x, slot_phi, w_in, b_in, w_out, b_out):
    me = lax.axis_index("seq")
    y, x, z, core = (c.astype(jnp.int32) for c in coords(me))
    mine = core * HALF
    to, got = targets(core, y, x, z)
    other_to, other_got = targets(1 - core, y, x, z)
    where = jnp.stack([core] + to + other_to + got + other_got)
    *sent, logits, dispatch, x_half = dispatch_call(where, clips_x, slot_phi)
    arrived = [swap_cores(piece) for piece in sent]
    own, stats = own_call(where, x_half, dispatch, sent)
    pieces = [send_piece(merge_cores_call(k, own, stats, arrived[k]), k) for k in SEND_ORDER[:3]]
    packed = merge_four_call([merge_cores_call(0, own, stats, arrived[0])] + pieces)
    packed = exchange(packed, STAGE_TWO)
    slot_in = merge_yz_call(packed).reshape(CLIPS * 4, HALF)
    partner = swap_cores(slot_in)
    rows = jnp.where(
        core == 0,
        jnp.concatenate([slot_in, partner], axis=1),
        jnp.concatenate([partner, slot_in], axis=1),
    )
    pre = jnp.dot(rows, w_in, preferred_element_type=F32)
    hidden = jax.nn.gelu(pre + b_in.astype(F32), approximate=False).astype(BF16)
    partial = jnp.dot(hidden, w_out, preferred_element_type=F32)
    part_mine = jnp.where(core == 0, partial[:, :HALF], partial[:, HALF:])
    part_theirs = jnp.where(core == 0, partial[:, HALF:], partial[:, :HALF])
    bias = lax.dynamic_slice(b_out, (me // 2, mine), (1, HALF)).astype(F32)
    summed = part_mine + swap_cores(part_theirs.astype(BF16)).astype(F32)
    slot_out = (summed + bias).astype(BF16)
    slot_out = slot_out.reshape(CLIPS, 4, HALF).transpose(1, 0, 2).reshape(1, 4, CLIPS * HALF)
    gathered = flatten_call(exchange(jnp.broadcast_to(slot_out, (16, 4, CLIPS * HALF)), STAGE_TWO))
    arriving = [send_piece(gathered, k) for k in SEND_ORDER[:3]]
    comb, other_comb, gathered = comb_call(where, logits, gathered)
    pieces = [gathered] + [arriving[SEND_ORDER.index(k)] for k in (1, 2, 3)]
    others = [swap_cores(piece) for piece in pieces]
    return mix_all_call(where, mix_own_call(comb, pieces), other_comb, others)


def solution(mesh):
    placed = (P("clip", "seq", None), P(), P(None, "seq"), P("seq"), P("seq", None), P())
    return jax.shard_map(
        per_device, mesh=mesh, in_specs=placed, out_specs=P("clip", "seq", None), check_vma=False
    )
```

time: 1760 us -> 92.1 us (0.05)
  waiting for transfers between devices: 1050 us -> 12.6 us
  blocking collectives: 658 us -> 42.8 us
    unnamed x3 -> x0, waiting for transfers between devices: 943 us -> none
    psum x1 -> x0, blocking collectives: 331 us -> none  [per_device(): col_total = lax.psum(jnp.sum(expo, axis=1), 'seq')]
    pmax x1 -> x0, blocking collectives: 328 us -> none  [per_device(): col_max = lax.pmax(local_max, 'seq')]
    all_gather x1 -> x0, waiting for transfers between devices: 106 us -> none  [per_device(): lax.all_gather(slot_out, 'seq', axis=0, tiled=True)]
    all_to_all x0 -> x2, blocking collectives: none -> 42.8 us  [exchange(): lax.all_to_all(value, 'seq', 0, 0, tiled=True, axis_index_groups=groups)]
  transfers between devices with their start and end apart: 4 -> 16, of which waited for: 4 -> 8; matrix products, arithmetic and copies ran while one was open for 0% -> 1% of each run, Pallas kernels for 0% -> 6%
where the time goes in v3:
time: 92.1 us; the launch traced here: 91.8 us
  blocking collectives  42.8 us (46%)
  starting transfers between devices  15.7 us (17%)
  Pallas kernels  13.8 us (15%)
  waiting for transfers between devices  12.6 us (14%)
  matrix products  3.11 us (3%)
  local copies, waits for them, and re-layouts  2.68 us (3%)
    all_to_all x2, blocking collectives, exchange(): lax.all_to_all(value, 'seq', 0, 0, tiled=True, axis_index_groups=groups)  42.8 us
    ppermute x6, waiting for transfers between devices, send_piece(): lax.ppermute(value, 'seq', [(source, peer(source, k)) for source in range...  10.7 us
    ppermute x6, starting transfers between devices, send_piece(): lax.ppermute(value, 'seq', [(source, peer(source, k)) for source in range...  8.61 us
    ppermute x10, starting transfers between devices, swap_cores(): lax.ppermute(value, 'seq', [(source, source ^ 1) for source in range(128)])  7.06 us
    pallas_call x1, Pallas kernels, dispatch_call(): pl.pallas_call(dispatch_kernel, out_shape=tuple((jax.ShapeDtypeStruct((64...  5.46 us
    dot_general x1, matrix products, per_device(): partial = jnp.dot(hidden, w_out, preferred_element_type=F32)  3.11 us
    unnamed x10, local copies, waits for them, and re-layouts  2.48 us
    pallas_call x1, Pallas kernels, mix_all_call(): pl.pallas_call(mix_all_kernel, out_shape=jax.ShapeDtypeStruct((CLIPS, TOK...  2.11 us
  transfers between devices with their start and end apart: 16, of which 8 were waited for; matrix products, arithmetic and copies ran while one was open for 1% of the time, Pallas kernels for 6%

profile of v3, /device:TPU:1, one launch (start us, length us, event | category | flops | bytes accessed | tf_op | source)
XLA Modules:
  0.0 91.8 jit_solution(1617360810083727521)
XLA Ops:
  0.1 1.2 %copy-done.3 = bf16[1280,256]{1,0:T(8,128)(2,1)S(1)} copy-done((bf16[1280,256]{1,0:T(8,128)(2,1)S(1)}, bf16[1280,256]{1,0:T(8,128)(2,1)}, u32[]{:S(2)}) %copy-start.3) | copy-done | bytes 655384
  1.3 5.5 %dispatch.1 = (bf16[64,2688]{1,0:T(8,128)(2,1)S(1)}, bf16[64,2688]{1,0:T(8,128)(2,1)S(1)}, bf16[64,2688]{1,0:T(8,128)(2,1)S(1)}, bf16[64,2688]{1,0:T(8,128)(2,1)...) custom-call(s32[17]{0:T(128)S(1)} %stack.59.where_ref, ...), custom_call_target="tpu_custom_call" | custom-call | flops 1006632960 | bytes 6291456 | tf_op jit(solution)/shard_map/dispatch/pallas_call | solution.py:164
  6.8 3.3 %collective-permute-start.1 = (bf16[64,2688]{1,0:T(8,128)(2,1)S(1)}, bf16[64,2688]{1,0:T(8,128)(2,1)S(1)}, u32[]{:S(2)}, u32[]{:S(2)}) collective-permute-start(bf16[64,2688]{1,0:T(8,128)(2,1)S(1)} %get-tuple-element.23.s3), channel_id=1, source_target_pairs={{0,1},{1,0},{2,3},{3,2},{4,5},{5,4},{6,7},{7,6},{8,9},{9,8},{10,11... | collective-permute-start | bytes 1032200 | tf_op jit(solution)/shard_map/ppermute | solution.py:51
  10.8 1.9 %own_half.1 = (f32[256,2560]{1,0:T(8,128)S(1)}, bf16[256,128]{1,0:T(8,128)(2,1)S(1)}) custom-call(s32[17]{0:T(128)S(1)} %stack.59.where_ref, bf16[4,256,640]{2,1,0:T(8,128)(2,1)S(1)} %get-tuple-element.18.x_ref, bf16[4,256,256]{2,1,0:T(8,128)(2,1)S(1)} %get-tuple-element.19.dispatch_ref, bf16[64,2688]{1,0:T(8,128)(2,1)S(1)} %get-tuple-element.20.s0, ...), custom_call_target="tpu_custom_call" | custom-call | flops 335544320 | bytes 6291456 | tf_op jit(solution)/shard_map/own_half/pallas_call | solution.py:199
  13.0 2.6 %collective-permute-start.2 = (bf16[64,2688]{1,0:T(8,128)(2,1)S(1)}, bf16[64,2688]{1,0:T(8,128)(2,1)S(1)}, u32[]{:S(2)}, u32[]{:S(2)}) collective-permute-start(bf16[64,2688]{1,0:T(8,128)(2,1)S(1)} %merge_cores.5), channel_id=1, source_target_pairs={{0,32},{1,67},{2,34},{3,65},{4,36},{5,71},{6,38},{7,69},{8,40},{9,... | collective-permute-start | bytes 1032200 | tf_op jit(solution)/shard_map/ppermute | solution.py:55
  16.4 1.7 %collective-permute-start.6 = (bf16[64,2688]{1,0:T(8,128)(2,1)S(1)}, bf16[64,2688]{1,0:T(8,128)(2,1)S(1)}, u32[]{:S(2)}, u32[]{:S(2)}) collective-permute-start(bf16[64,2688]{1,0:T(8,128)(2,1)S(1)} %merge_cores.7), channel_id=1, source_target_pairs={{0,48},{1,65},{2,50},{3,67},{4,52},{5,69},{6,54},{7,71},{8,56},{9,... | collective-permute-start | bytes 1032200 | tf_op jit(solution)/shard_map/ppermute | solution.py:55
  18.4 3.3 %collective-permute-done.2.refs_1_ = bf16[64,2688]{1,0:T(8,128)(2,1)S(1)} collective-permute-done((bf16[64,2688]{1,0:T(8,128)(2,1)S(1)}, bf16[64,2688]{1,0:T(8,128)(2,1)S(1)}, u32[]{:S(2)}, u32[]{:S(2)}) %collective-permute-start.2) | collective-permute-done | bytes 344096 | tf_op jit(solution)/shard_map/ppermute | solution.py:55
  21.7 2.4 %collective-permute-done.4.refs_2_ = bf16[64,2688]{1,0:T(8,128)(2,1)S(1)} collective-permute-done((bf16[64,2688]{1,0:T(8,128)(2,1)S(1)}, bf16[64,2688]{1,0:T(8,128)(2,1)S(1)}, u32[]{:S(2)}, u32[]{:S(2)}) %collective-permute-start.4) | collective-permute-done | bytes 344096 | tf_op jit(solution)/shard_map/ppermute | solution.py:55
  24.1 1.2 %collective-permute-done.6.refs_3_ = bf16[64,2688]{1,0:T(8,128)(2,1)S(1)} collective-permute-done((bf16[64,2688]{1,0:T(8,128)(2,1)S(1)}, bf16[64,2688]{1,0:T(8,128)(2,1)S(1)}, u32[]{:S(2)}, u32[]{:S(2)}) %collective-permute-start.6) | collective-permute-done | bytes 344096 | tf_op jit(solution)/shard_map/ppermute | solution.py:55
  25.3 0.6 merge_four.1
  25.9 22.6 %all_to_all.10.value_ref = bf16[16,4,2688]{2,1,0:T(4,128)(2,1)S(1)} all-to-all(bf16[16,4,2688]{2,1,0:T(4,128)(2,1)S(1)} %merge_four.1), channel_id=1, replica_groups={{0,2,4,6,8,10,12,14,64,66,68,70,72,74,76,78},{1,5,9,13,17,21,25,29,33,3..., dimensions={0} | all-to-all | bytes 688128 | tf_op jit(solution)/shard_map/all_to_all | solution.py:47
  48.9 1.4 %collective-permute-start.7 = (bf16[16,640]{1,0:T(8,128)(2,1)S(1)}, bf16[16,640]{1,0:T(8,128)(2,1)S(1)}, u32[]{:S(2)}, u32[]{:S(2)}) collective-permute-start(bf16[16,640]{1,0:T(8,128)(2,1)S(1)} %reshape.9), channel_id=1, source_target_pairs={{0,1},{1,0},{2,3},{3,2},{4,5},{5,4},{6,7},{7,6},{8,9},{9,8},{10,11... | collective-permute-start | bytes 61448 | tf_op jit(solution)/shard_map/ppermute | solution.py:51
  50.3 0.8 collective-permute-done.7
  51.2 3.1 %fusion.10 = f32[16,1280]{1,0:T(8,128)S(1)} fusion(bf16[1280,1280]{1,0:T(8,128)(2,1)S(1)} %copy-done, bf16[1280,1280]{1,0:T(8,128)(2,1)} %param.8, bf16[16,640]{1,0:T(8,128)(2,1)S(1)} %collective-permute-done.7, bf16[16,640]{1,0:T(8,128)(2,1)S(1)} %reshape.9, f32[1280]{0:T(1024)S(1)} %convert_element_type.16, pred[]{:T(512)S(6)} %eq.45), kind=kOutput, calls=%fused_computation.20 | convolution fusion | flops 106393600 | bytes 6681601 | tf_op jit(solution)/shard_map/dot_general | solution.py:441
  54.3 0.6 collective-permute-start.8
  54.9 0.8 convert_reduce_fusion
  55.9 20.1 %all_to_all.11.value_ref = bf16[16,4,2560]{2,1,0:T(4,128)(2,1)S(1)} all-to-all(bf16[16,4,2560]{2,1,0:T(4,128)(2,1)S(1)} %broadcast_in_dim.9), channel_id=1, replica_groups={{0,2,4,6,8,10,12,14,64,66,68,70,72,74,76,78},{1,5,9,13,17,21,25,29,33,3..., dimensions={0} | all-to-all | bytes 655360 | tf_op jit(solution)/shard_map/all_to_all | solution.py:47
  76.8 3.5 %collective-permute-start.11 = (bf16[64,2560]{1,0:T(8,128)(2,1)S(1)}, bf16[64,2560]{1,0:T(8,128)(2,1)S(1)}, u32[]{:S(2)}, u32[]{:S(2)}) collective-permute-start(bf16[64,2560]{1,0:T(8,128)(2,1)S(1)} %flatten.1.piece_ref), channel_id=1, source_target_pairs={{0,32},{1,67},{2,34},{3,65},{4,36},{5,71},{6,38},{7,69},{8,40},{9,... | collective-permute-start | bytes 983048 | tf_op jit(solution)/shard_map/ppermute | solution.py:55
  80.3 1.2 %copy-done.2 = f32[4,256,256]{2,1,0:T(8,128)S(1)} copy-done((f32[4,256,256]{2,1,0:T(8,128)S(1)}, f32[4,256,256]{2,1,0:T(8,128)}, u32[]{:S(2)}) %copy-start.2) | copy-done | bytes 1048600
  81.5 1.5 %comb.1 = (bf16[4,256,256]{2,1,0:T(8,128)(2,1)S(1)}, bf16[4,256,256]{2,1,0:T(8,128)(2,1)S(1)}, bf16[64,2560]{1,0:T(8,128)(2,1)S(1)}) custom-call(s32[17]{0:T(128)S(1)} %stack.59.where_ref, f32[4,256,256]{2,1,0:T(8,128)S(1)} %copy-done.2, bf16[64,2560]{1,0:T(8,128)(2,1)S(1)} %flatten.1.piece_ref), custom_call_target="tpu_custom_call" | custom-call | flops 134217728 | bytes 4194304 | tf_op jit(solution)/shard_map/comb/pallas_call | solution.py:227
  83.6 3.8 %collective-permute-done.10.p2 = bf16[64,2560]{1,0:T(8,128)(2,1)S(1)} collective-permute-done((bf16[64,2560]{1,0:T(8,128)(2,1)S(1)}, bf16[64,2560]{1,0:T(8,128)(2,1)S(1)}, u32[]{:S(2)}, u32[]{:S(2)}) %collective-permute-start.10) | collective-permute-done | bytes 327712 | tf_op jit(solution)/shard_map/ppermute | solution.py:55
  87.9 0.6 mix_own.1.own_ref
  88.5 0.5 collective-permute-done.14.p2
  89.5 2.1 %mix_all.1 = bf16[4,256,1280]{2,1,0:T(8,128)(2,1)} custom-call(s32[17]{0:T(128)S(1)} %stack.59.where_ref, bf16[4,256,640]{2,1,0:T(8,128)(2,1)S(1)} %mix_own.1.own_ref, bf16[4,256,256]{2,1,0:T(8,128)(2,1)S(1)} %get-tuple-element.28.comb_ref, bf16[64,2560]{1,0:T(8,128)(2,1)S(1)} %collective-permute-done.12.p0, ...), custom_call_target="tpu_custom_call" | custom-call | flops 335544320 | bytes 6291456 | tf_op jit(solution)/shard_map/mix_all/pallas_call | solution.py:396
  (41 shorter events, 4.9 us)
Async XLA Ops:
  0.0 51.2 %copy-start = (bf16[1280,1280]{1,0:T(8,128)(2,1)S(1)}, bf16[1280,1280]{1,0:T(8,128)(2,1)}, u32[]{:S(2)}) copy-start(bf16[1280,1280]{1,0:T(8,128)(2,1)} %param.10) | copy-start | bytes 9830404
  0.1 1.2 %copy-start.3 = (bf16[1280,256]{1,0:T(8,128)(2,1)S(1)}, bf16[1280,256]{1,0:T(8,128)(2,1)}, u32[]{:S(2)}) copy-start(bf16[1280,256]{1,0:T(8,128)(2,1)} %phi_hbm.1) | copy-start | bytes 1966084
  6.8 6.2 %copy-start.1 = (f32[4,256,256]{2,1,0:T(8,128)}, f32[4,256,256]{2,1,0:T(8,128)S(1)}, u32[]{:S(2)}) copy-start(f32[4,256,256]{2,1,0:T(8,128)S(1)} %get-tuple-element.17.logits_ref) | copy-start | bytes 3145732
  6.8 5.9 %collective-permute-start.1 = (bf16[64,2688]{1,0:T(8,128)(2,1)S(1)}, bf16[64,2688]{1,0:T(8,128)(2,1)S(1)}, u32[]{:S(2)}, u32[]{:S(2)}) collective-permute-start(bf16[64,2688]{1,0:T(8,128)(2,1)S(1)} %get-tuple-element.23.s3), channel_id=1, source_target_pairs={{0,1},{1,0},{2,3},{3,2},{4,5},{5,4},{6,7},{7,6},{8,9},{9,8},{10,11... | collective-permute-start | bytes 1032200 | tf_op jit(solution)/shard_map/ppermute | solution.py:51
  10.2 5.5 %collective-permute-start.3 = (bf16[64,2688]{1,0:T(8,128)(2,1)S(1)}, bf16[64,2688]{1,0:T(8,128)(2,1)S(1)}, u32[]{:S(2)}, u32[]{:S(2)}) collective-permute-start(bf16[64,2688]{1,0:T(8,128)(2,1)S(1)} %get-tuple-element.21.s1), channel_id=1, source_target_pairs={{0,1},{1,0},{2,3},{3,2},{4,5},{5,4},{6,7},{7,6},{8,9},{9,8},{10,11... | collective-permute-start | bytes 1032200 | tf_op jit(solution)/shard_map/ppermute | solution.py:51
  10.3 5.8 %collective-permute-start.5 = (bf16[64,2688]{1,0:T(8,128)(2,1)S(1)}, bf16[64,2688]{1,0:T(8,128)(2,1)S(1)}, u32[]{:S(2)}, u32[]{:S(2)}) collective-permute-start(bf16[64,2688]{1,0:T(8,128)(2,1)S(1)} %get-tuple-element.22.s2), channel_id=1, source_target_pairs={{0,1},{1,0},{2,3},{3,2},{4,5},{5,4},{6,7},{7,6},{8,9},{9,8},{10,11... | collective-permute-start | bytes 1032200 | tf_op jit(solution)/shard_map/ppermute | solution.py:51
  10.7 7.4 %collective-permute-start = (bf16[64,2688]{1,0:T(8,128)(2,1)S(1)}, bf16[64,2688]{1,0:T(8,128)(2,1)S(1)}, u32[]{:S(2)}, u32[]{:S(2)}) collective-permute-start(bf16[64,2688]{1,0:T(8,128)(2,1)S(1)} %get-tuple-element.20.s0), channel_id=1, source_target_pairs={{0,1},{1,0},{2,3},{3,2},{4,5},{5,4},{6,7},{7,6},{8,9},{9,8},{10,11... | collective-permute-start | bytes 1032200 | tf_op jit(solution)/shard_map/ppermute | solution.py:51
  13.0 8.7 %collective-permute-start.2 = (bf16[64,2688]{1,0:T(8,128)(2,1)S(1)}, bf16[64,2688]{1,0:T(8,128)(2,1)S(1)}, u32[]{:S(2)}, u32[]{:S(2)}) collective-permute-start(bf16[64,2688]{1,0:T(8,128)(2,1)S(1)} %merge_cores.5), channel_id=1, source_target_pairs={{0,32},{1,67},{2,34},{3,65},{4,36},{5,71},{6,38},{7,69},{8,40},{9,... | collective-permute-start | bytes 1032200 | tf_op jit(solution)/shard_map/ppermute | solution.py:55
  16.0 8.1 %collective-permute-start.4 = (bf16[64,2688]{1,0:T(8,128)(2,1)S(1)}, bf16[64,2688]{1,0:T(8,128)(2,1)S(1)}, u32[]{:S(2)}, u32[]{:S(2)}) collective-permute-start(bf16[64,2688]{1,0:T(8,128)(2,1)S(1)} %merge_cores.6), channel_id=1, source_target_pairs={{0,16},{1,3},{2,18},{3,1},{4,20},{5,7},{6,22},{7,5},{8,24},{9,11},... | collective-permute-start | bytes 1032200 | tf_op jit(solution)/shard_map/ppermute | solution.py:55
  16.4 33.9 %copy-start.4 = (bf16[1280]{0:T(1024)(128)(2,1)S(1)}, bf16[1280]{0:T(1024)(128)(2,1)}, u32[]{:S(2)}) copy-start(bf16[1280]{0:T(1024)(128)(2,1)} %param.9) | copy-start | bytes 7684
  16.4 8.9 %collective-permute-start.6 = (bf16[64,2688]{1,0:T(8,128)(2,1)S(1)}, bf16[64,2688]{1,0:T(8,128)(2,1)S(1)}, u32[]{:S(2)}, u32[]{:S(2)}) collective-permute-start(bf16[64,2688]{1,0:T(8,128)(2,1)S(1)} %merge_cores.7), channel_id=1, source_target_pairs={{0,48},{1,65},{2,50},{3,67},{4,52},{5,69},{6,54},{7,71},{8,56},{9,... | collective-permute-start | bytes 1032200 | tf_op jit(solution)/shard_map/ppermute | solution.py:55
  48.9 2.3 %collective-permute-start.7 = (bf16[16,640]{1,0:T(8,128)(2,1)S(1)}, bf16[16,640]{1,0:T(8,128)(2,1)S(1)}, u32[]{:S(2)}, u32[]{:S(2)}) collective-permute-start(bf16[16,640]{1,0:T(8,128)(2,1)S(1)} %reshape.9), channel_id=1, source_target_pairs={{0,1},{1,0},{2,3},{3,2},{4,5},{5,4},{6,7},{7,6},{8,9},{9,8},{10,11... | collective-permute-start | bytes 61448 | tf_op jit(solution)/shard_map/ppermute | solution.py:51
  54.3 1.5 %collective-permute-start.8 = (bf16[16,640]{1,0:T(8,128)(2,1)S(1)}, bf16[16,640]{1,0:T(8,128)(2,1)S(1)}, u32[]{:S(2)}, u32[]{:S(2)}) collective-permute-start(bf16[16,640]{1,0:T(8,128)(2,1)S(1)} %select_convert_fusion), channel_id=1, source_target_pairs={{0,1},{1,0},{2,3},{3,2},{4,5},{5,4},{6,7},{7,6},{8,9},{9,8},{10,11... | collective-permute-start | bytes 61448 | tf_op jit(solution)/shard_map/ppermute | solution.py:51
  76.1 7.0 %collective-permute-start.9 = (bf16[64,2560]{1,0:T(8,128)(2,1)S(1)}, bf16[64,2560]{1,0:T(8,128)(2,1)S(1)}, u32[]{:S(2)}, u32[]{:S(2)}) collective-permute-start(bf16[64,2560]{1,0:T(8,128)(2,1)S(1)} %flatten.1.piece_ref), channel_id=1, source_target_pairs={{0,16},{1,3},{2,18},{3,1},{4,20},{5,7},{6,22},{7,5},{8,24},{9,11},... | collective-permute-start | bytes 983048 | tf_op jit(solution)/shard_map/ppermute | solution.py:55
  76.4 10.9 %collective-permute-start.10 = (bf16[64,2560]{1,0:T(8,128)(2,1)S(1)}, bf16[64,2560]{1,0:T(8,128)(2,1)S(1)}, u32[]{:S(2)}, u32[]{:S(2)}) collective-permute-start(bf16[64,2560]{1,0:T(8,128)(2,1)S(1)} %flatten.1.piece_ref), channel_id=1, source_target_pairs={{0,48},{1,65},{2,50},{3,67},{4,52},{5,69},{6,54},{7,71},{8,56},{9,... | collective-permute-start | bytes 983048 | tf_op jit(solution)/shard_map/ppermute | solution.py:55
  76.8 10.6 %collective-permute-start.11 = (bf16[64,2560]{1,0:T(8,128)(2,1)S(1)}, bf16[64,2560]{1,0:T(8,128)(2,1)S(1)}, u32[]{:S(2)}, u32[]{:S(2)}) collective-permute-start(bf16[64,2560]{1,0:T(8,128)(2,1)S(1)} %flatten.1.piece_ref), channel_id=1, source_target_pairs={{0,32},{1,67},{2,34},{3,65},{4,36},{5,71},{6,38},{7,69},{8,40},{9,... | collective-permute-start | bytes 983048 | tf_op jit(solution)/shard_map/ppermute | solution.py:55
  80.3 1.2 %copy-start.2 = (f32[4,256,256]{2,1,0:T(8,128)S(1)}, f32[4,256,256]{2,1,0:T(8,128)}, u32[]{:S(2)}) copy-start(f32[4,256,256]{2,1,0:T(8,128)} %copy-done.1) | copy-start | bytes 3145732
  83.0 5.5 %collective-permute-start.12 = (bf16[64,2560]{1,0:T(8,128)(2,1)S(1)}, bf16[64,2560]{1,0:T(8,128)(2,1)S(1)}, u32[]{:S(2)}, u32[]{:S(2)}) collective-permute-start(bf16[64,2560]{1,0:T(8,128)(2,1)S(1)} %get-tuple-element.27.p0), channel_id=1, source_target_pairs={{0,1},{1,0},{2,3},{3,2},{4,5},{5,4},{6,7},{7,6},{8,9},{9,8},{10,11... | collective-permute-start | bytes 983048 | tf_op jit(solution)/shard_map/ppermute | solution.py:51
  83.1 5.4 %collective-permute-start.13 = (bf16[64,2560]{1,0:T(8,128)(2,1)S(1)}, bf16[64,2560]{1,0:T(8,128)(2,1)S(1)}, u32[]{:S(2)}, u32[]{:S(2)}) collective-permute-start(bf16[64,2560]{1,0:T(8,128)(2,1)S(1)} %collective-permute-done.9.p1), channel_id=1, source_target_pairs={{0,1},{1,0},{2,3},{3,2},{4,5},{5,4},{6,7},{7,6},{8,9},{9,8},{10,11... | collective-permute-start | bytes 983048 | tf_op jit(solution)/shard_map/ppermute | solution.py:51
  87.4 1.6 %collective-permute-start.14 = (bf16[64,2560]{1,0:T(8,128)(2,1)S(1)}, bf16[64,2560]{1,0:T(8,128)(2,1)S(1)}, u32[]{:S(2)}, u32[]{:S(2)}) collective-permute-start(bf16[64,2560]{1,0:T(8,128)(2,1)S(1)} %collective-permute-done.10.p2), channel_id=1, source_target_pairs={{0,1},{1,0},{2,3},{3,2},{4,5},{5,4},{6,7},{7,6},{8,9},{9,8},{10,11... | collective-permute-start | bytes 983048 | tf_op jit(solution)/shard_map/ppermute | solution.py:51
  87.4 2.1 %collective-permute-start.15 = (bf16[64,2560]{1,0:T(8,128)(2,1)S(1)}, bf16[64,2560]{1,0:T(8,128)(2,1)S(1)}, u32[]{:S(2)}, u32[]{:S(2)}) collective-permute-start(bf16[64,2560]{1,0:T(8,128)(2,1)S(1)} %collective-permute-done.11.p3), channel_id=1, source_target_pairs={{0,1},{1,0},{2,3},{3,2},{4,5},{5,4},{6,7},{7,6},{8,9},{9,8},{10,11... | collective-permute-start | bytes 983048 | tf_op jit(solution)/shard_map/ppermute | solution.py:51

commit v4 on v3

--- a/solution.py
+++ b/solution.py
@@ -2,6 +2,7 @@
 
 import jax
 import jax.numpy as jnp
+import numpy as np
 from jax import lax
 from jax.experimental import pallas as pl
 from jax.experimental.pallas import tpu as pltpu
@@ -13,11 +14,13 @@
 SLOTS = 256
 TOK = 256
 D = 1280
+EXPERTS = 64
 HALF = 640
 STATS = CLIPS * HALF
 ROW = STATS + 128
 VMEM_LIMIT = 8 * 2**20
-DISPATCH_VMEM = 49 * 2**20
+LOAD_VMEM = 49 * 2**20
+DISPATCH_VMEM = 16 * 2**20
 
 
 def coords(index):
@@ -61,9 +64,6 @@
 
 def cost(flops, bytes_accessed):
     return pl.CostEstimate(flops=flops, bytes_accessed=bytes_accessed, transcendentals=0)
-
-
-DISPATCH_COST = cost(2 * 1024 * 256 * 1920, 6 * 2**20)
 
 
 def stats_lanes(clip, peak, total):
@@ -115,72 +115,79 @@
 VMEM_SPEC = pl.BlockSpec(memory_space=pltpu.VMEM)
 SMEM_SPEC = pl.BlockSpec(memory_space=pltpu.SMEM)
 HBM_SPEC = pl.BlockSpec(memory_space=pltpu.HBM)
-SENT, OTHER_SENT, GOT, OTHER_GOT = 1, 5, 9, 13
+SENT, OTHER_SENT, GOT, OTHER_GOT, EXPERT = 1, 5, 9, 13, 17
 SEND_ORDER = (3, 1, 2, 0)
 
 
-def dispatch_kernel(where_ref, x_hbm, phi_hbm, *refs):
-    send_refs, (logits_ref, dispatch_ref, x_ref, other_ref, phi_ref, x_sem, phi_sem) = refs[:4], refs[4:]
-    core = where_ref[0]
-    phi_copy = pltpu.make_async_copy(phi_hbm, phi_ref, phi_sem)
-    phi_copy.start()
+def load_kernel(x_hbm, x_ref, sem):
+    rows = TOK // 2
     copies = []
-    for clip in range(CLIPS):
-        for side, target in ((core, x_ref), (1 - core, other_ref)):
-            source = x_hbm.at[clip, :, dynamic_half(side)]
-            copies.append(pltpu.make_async_copy(source, target.at[clip], x_sem.at[len(copies)]))
-            copies[-1].start()
-    order = order_matrix(1 - core, where_ref, OTHER_SENT)
-    phi_copy.wait()
-    phi = jnp.concatenate([phi_ref[phi_rows(core), :], phi_ref[phi_rows(1 - core), :]], axis=0)
+    for k in range(2 * CLIPS):
+        at = (k // 2, pl.ds(k % 2 * rows, rows))
+        copies.append(pltpu.make_async_copy(x_hbm.at[at], x_ref.at[at], sem.at[k]))
+        copies[k].start()
     for copy in copies:
         copy.wait()
-    tokens = jnp.concatenate(
-        [x_ref[...].reshape(CLIPS * TOK, HALF), other_ref[...].reshape(CLIPS * TOK, HALF)], axis=1
-    )
-    all_logits = jnp.dot(tokens, phi, preferred_element_type=F32)
+
+
+def load_call(clips_x):
+    return pl.pallas_call(
+        load_kernel,
+        out_shape=jax.ShapeDtypeStruct((CLIPS, TOK, D), BF16),
+        in_specs=[HBM_SPEC],
+        out_specs=VMEM_SPEC,
+        scratch_shapes=[pltpu.SemaphoreType.DMA((2 * CLIPS,))],
+        compiler_params=params(LOAD_VMEM),
+        cost_estimate=cost(0, 6 * 2**20),
+        name="load",
+    )(clips_x)
+
+
+def dispatch_kernel(where_ref, x_ref, phi_ref, *refs):
+    send_refs, (logits_ref, dispatch_ref) = refs[:4], refs[4:]
+    core = where_ref[0]
+    order = order_matrix(1 - core, where_ref, OTHER_SENT)
+    tokens = x_ref[...].reshape(CLIPS * TOK, D)
+    all_logits = jnp.dot(tokens, phi_ref[...], preferred_element_type=F32)
     stats = jnp.zeros((SLOTS, 128), F32)
+    rounded = []
     for clip in range(CLIPS):
         logits = all_logits[clip * TOK : clip * TOK + TOK]
         logits_ref[clip] = logits
         peak = jnp.max(logits, axis=0, keepdims=True)
         expo = jnp.exp(logits - peak)
         total = jnp.sum(expo, axis=0, keepdims=True)
-        dispatch = lax.dot_general(
-            order, expo.astype(BF16), (((1,), (1,)), ((), ())), preferred_element_type=F32
-        ).astype(BF16)
-        dispatch_ref[clip] = dispatch
-        sums = jnp.dot(dispatch, other_ref[clip], preferred_element_type=F32).astype(BF16)
+        rounded.append(expo.astype(BF16))
+        both = jnp.concatenate([peak, total, jnp.zeros((6, SLOTS), F32)], axis=0).T
+        stats += stats_lanes(clip, both[:, 0:1], both[:, 1:2])
+    dispatch = lax.dot_general(
+        order, jnp.concatenate(rounded, axis=0), (((1,), (1,)), ((), ())), preferred_element_type=F32
+    ).astype(BF16)
+    dispatch_ref[...] = dispatch
+    for clip in range(CLIPS):
+        part = dispatch[:, clip * TOK : clip * TOK + TOK]
+        sums = jnp.dot(part, x_ref[clip, :, dynamic_half(1 - core)], preferred_element_type=F32).astype(BF16)
         for k in range(4):
             send_refs[k][:, column_slice(clip)] = sums[k * 64 : k * 64 + 64]
-        both = jnp.concatenate([peak, total, jnp.zeros((6, SLOTS), F32)], axis=0).T
-        stats += stats_lanes(clip, both[:, 0:1], both[:, 1:2])
     stats = jnp.dot(order, stats.astype(BF16), preferred_element_type=F32).astype(BF16)
     for k in range(4):
         send_refs[k][:, STATS:] = stats[k * 64 : k * 64 + 64]
 
 
-def dispatch_call(where, clips_x, slot_phi):
+def dispatch_call(where, x, slot_phi):
     return pl.pallas_call(
         dispatch_kernel,
         out_shape=tuple(jax.ShapeDtypeStruct((64, ROW), BF16) for _ in range(4))
         + (
             jax.ShapeDtypeStruct((CLIPS, TOK, SLOTS), F32),
-            jax.ShapeDtypeStruct((CLIPS, SLOTS, TOK), BF16),
-            jax.ShapeDtypeStruct((CLIPS, TOK, HALF), BF16),
+            jax.ShapeDtypeStruct((SLOTS, CLIPS * TOK), BF16),
         ),
-        in_specs=[SMEM_SPEC, HBM_SPEC, HBM_SPEC],
-        out_specs=(VMEM_SPEC,) * 7,
-        scratch_shapes=[
-            pltpu.VMEM((CLIPS, TOK, HALF), BF16),
-            pltpu.VMEM((D, SLOTS), BF16),
-            pltpu.SemaphoreType.DMA((2 * CLIPS,)),
-            pltpu.SemaphoreType.DMA,
-        ],
+        in_specs=[SMEM_SPEC] + [VMEM_SPEC] * 2,
+        out_specs=(VMEM_SPEC,) * 6,
         compiler_params=params(DISPATCH_VMEM),
-        cost_estimate=DISPATCH_COST,
+        cost_estimate=cost(2 * 1024 * 256 * 1920, 6 * 2**20),
         name="dispatch",
-    )(where, clips_x, slot_phi)
+    )(where, x, slot_phi)
 
 
 def own_kernel(where_ref, x_ref, dispatch_ref, s0, s1, s2, s3, own_ref, stats_ref):
@@ -190,12 +197,13 @@
     order = lax.dot_general(order, given, (((1,), (1,)), ((), ())), preferred_element_type=F32).astype(BF16)
     stats = jnp.concatenate([s[:, STATS:] for s in (s0, s1, s2, s3)], axis=0)
     stats_ref[...] = jnp.dot(order, stats, preferred_element_type=F32).astype(BF16)
-    for clip in range(CLIPS):
-        dispatch = jnp.dot(order, dispatch_ref[clip], preferred_element_type=F32).astype(BF16)
-        own_ref[:, column_slice(clip)] = jnp.dot(dispatch, x_ref[clip], preferred_element_type=F32)
-
-
-def own_call(where, x_half, dispatch, sent):
+    dispatch = jnp.dot(order, dispatch_ref[...], preferred_element_type=F32).astype(BF16)
+    for clip in range(CLIPS):
+        part = dispatch[:, clip * TOK : clip * TOK + TOK]
+        own_ref[:, column_slice(clip)] = jnp.dot(part, x_ref[clip, :, dynamic_half(core)], preferred_element_type=F32)
+
+
+def own_call(where, x, dispatch, sent):
     return pl.pallas_call(
         own_kernel,
         out_shape=(
@@ -207,7 +215,7 @@
         compiler_params=params(),
         cost_estimate=cost(2 * 1024 * 256 * 640, 6 * 2**20),
         name="own_half",
-    )(where, x_half, dispatch, *sent)
+    )(where, x, dispatch, *sent)
 
 
 def comb_kernel(where_ref, logits_ref, piece_ref, comb_ref, other_comb_ref, same_ref):
@@ -237,6 +245,52 @@
         cost_estimate=cost(2**27, 4 * 2**20),
         name="comb",
     )(where, logits, piece)
+
+
+def expert_in_kernel(where_ref, slot_in_ref, partner_ref, w_ref, b_ref, hidden_ref):
+    core = where_ref[0]
+    pre = jnp.dot(slot_in_ref[...], w_ref[phi_rows(core), :], preferred_element_type=F32)
+    pre += jnp.dot(partner_ref[...], w_ref[phi_rows(1 - core), :], preferred_element_type=F32)
+    pre += b_ref[...].astype(F32)
+    hidden_ref[...] = (0.5 * pre * (1.0 + lax.erf(pre * np.float32(np.sqrt(0.5))))).astype(BF16)
+
+
+def expert_in_call(where, slot_in, partner, w_in, b_in):
+    return pl.pallas_call(
+        expert_in_kernel,
+        out_shape=jax.ShapeDtypeStruct((CLIPS * 4, D), BF16),
+        in_specs=[SMEM_SPEC] + [VMEM_SPEC] * 4,
+        out_specs=VMEM_SPEC,
+        compiler_params=params(),
+        cost_estimate=cost(2 * 16 * D * D, 4 * 2**20),
+        name="expert_in",
+    )(where, slot_in, partner, w_in, b_in)
+
+
+def expert_out_kernel(where_ref, hidden_ref, w_ref, b_ref, mine_ref, theirs_ref):
+    core = where_ref[0]
+    hidden = hidden_ref[...]
+    expert = lax.broadcasted_iota(jnp.int32, (CLIPS * 4, EXPERTS), 1) == where_ref[EXPERT]
+    bias = jnp.dot(
+        jnp.where(expert, 1.0, 0.0).astype(BF16), b_ref[:, dynamic_half(core)], preferred_element_type=F32
+    )
+    theirs_ref[...] = jnp.dot(hidden, w_ref[:, dynamic_half(1 - core)], preferred_element_type=F32).astype(BF16)
+    mine_ref[...] = jnp.dot(hidden, w_ref[:, dynamic_half(core)], preferred_element_type=F32) + bias
+
+
+def expert_out_call(where, hidden, w_out, b_out):
+    return pl.pallas_call(
+        expert_out_kernel,
+        out_shape=(
+            jax.ShapeDtypeStruct((CLIPS * 4, HALF), F32),
+            jax.ShapeDtypeStruct((CLIPS * 4, HALF), BF16),
+        ),
+        in_specs=[SMEM_SPEC] + [VMEM_SPEC] * 3,
+        out_specs=(VMEM_SPEC,) * 2,
+        compiler_params=params(),
+        cost_estimate=cost(2 * 16 * D * D, 4 * 2**20),
+        name="expert_out",
+    )(where, hidden, w_out, b_out)
 
 
 def merge_cores_kernel(k, own_ref, mine_ref, arrived_ref, out_ref):
@@ -419,31 +473,21 @@
 def per_device(clips_x, slot_phi, w_in, b_in, w_out, b_out):
     me = lax.axis_index("seq")
     y, x, z, core = (c.astype(jnp.int32) for c in coords(me))
-    mine = core * HALF
     to, got = targets(core, y, x, z)
     other_to, other_got = targets(1 - core, y, x, z)
-    where = jnp.stack([core] + to + other_to + got + other_got)
-    *sent, logits, dispatch, x_half = dispatch_call(where, clips_x, slot_phi)
+    where = jnp.stack([core] + to + other_to + got + other_got + [(me // 2).astype(jnp.int32)])
+    tokens = load_call(clips_x)
+    *sent, logits, dispatch = dispatch_call(where, tokens, slot_phi)
     arrived = [swap_cores(piece) for piece in sent]
-    own, stats = own_call(where, x_half, dispatch, sent)
+    own, stats = own_call(where, tokens, dispatch, sent)
     pieces = [send_piece(merge_cores_call(k, own, stats, arrived[k]), k) for k in SEND_ORDER[:3]]
     packed = merge_four_call([merge_cores_call(0, own, stats, arrived[0])] + pieces)
     packed = exchange(packed, STAGE_TWO)
     slot_in = merge_yz_call(packed).reshape(CLIPS * 4, HALF)
     partner = swap_cores(slot_in)
-    rows = jnp.where(
-        core == 0,
-        jnp.concatenate([slot_in, partner], axis=1),
-        jnp.concatenate([partner, slot_in], axis=1),
-    )
-    pre = jnp.dot(rows, w_in, preferred_element_type=F32)
-    hidden = jax.nn.gelu(pre + b_in.astype(F32), approximate=False).astype(BF16)
-    partial = jnp.dot(hidden, w_out, preferred_element_type=F32)
-    part_mine = jnp.where(core == 0, partial[:, :HALF], partial[:, HALF:])
-    part_theirs = jnp.where(core == 0, partial[:, HALF:], partial[:, :HALF])
-    bias = lax.dynamic_slice(b_out, (me // 2, mine), (1, HALF)).astype(F32)
-    summed = part_mine + swap_cores(part_theirs.astype(BF16)).astype(F32)
-    slot_out = (summed + bias).astype(BF16)
+    hidden = expert_in_call(where, slot_in, partner, w_in, b_in[None])
+    part_mine, part_theirs = expert_out_call(where, hidden, w_out, b_out)
+    slot_out = (part_mine + swap_cores(part_theirs).astype(F32)).astype(BF16)
     slot_out = slot_out.reshape(CLIPS, 4, HALF).transpose(1, 0, 2).reshape(1, 4, CLIPS * HALF)
     gathered = flatten_call(exchange(jnp.broadcast_to(slot_out, (16, 4, CLIPS * HALF)), STAGE_TWO))
     arriving = [send_piece(gathered, k) for k in SEND_ORDER[:3]]

time: 92.1 us -> 89.3 us (0.970)
  matrix products: 3.11 us -> 0 us
  local copies, waits for them, and re-layouts: 2.68 us -> 0.27 us
  waiting for transfers between devices: 12.6 us -> 14.7 us
  Pallas kernels: 13.8 us -> 15.5 us
    pallas_call x0 -> x3, Pallas kernels: none -> 3.99 us  [the longest x1 1.8 us: load_call(): pl.pallas_call(load_kernel, out_shape=jax.ShapeDtypeStruct((CLIPS, TOK, D...]
    dot_general x1 -> x0, matrix products: 3.11 us -> none  [per_device(): partial = jnp.dot(hidden, w_out, preferred_element_type=F32)]
    unnamed x10 -> x14, local copies, waits for them, and re-layouts: 2.48 us -> 0.04 us
    pallas_call x1, Pallas kernels: 5.46 us -> 3.41 us  [dispatch_call(): pl.pallas_call(dispatch_kernel, out_shape=tuple((jax.ShapeDtypeStruct((64...]
    ppermute x6, waiting for transfers between devices: 10.7 us -> 12 us  [send_piece(): lax.ppermute(value, 'seq', [(source, peer(source, k)) for source in range...]
  transfers between devices with their start and end apart: 16 -> 16, of which waited for: 8 -> 9; matrix products, arithmetic and copies ran while one was open for 1% -> 0% of each run, Pallas kernels for 6% -> 6%
where the time goes in v4:
time: 89.3 us; the launch traced here: 89.1 us
  blocking collectives  42.9 us (48%)
  Pallas kernels  15.5 us (17%)
  starting transfers between devices  15.3 us (17%)
  waiting for transfers between devices  14.7 us (16%)
    all_to_all x2, blocking collectives, exchange(): lax.all_to_all(value, 'seq', 0, 0, tiled=True, axis_index_groups=groups)  42.9 us
    ppermute x6, waiting for transfers between devices, send_piece(): lax.ppermute(value, 'seq', [(source, peer(source, k)) for source in range...  12 us
    ppermute x6, starting transfers between devices, send_piece(): lax.ppermute(value, 'seq', [(source, peer(source, k)) for source in range...  8.61 us
    ppermute x10, starting transfers between devices, swap_cores(): lax.ppermute(value, 'seq', [(source, source ^ 1) for source in range(128)])  6.73 us
    pallas_call x1, Pallas kernels, dispatch_call(): pl.pallas_call(dispatch_kernel, out_shape=tuple((jax.ShapeDtypeStruct((64...  3.41 us
    ppermute x10, waiting for transfers between devices, swap_cores(): lax.ppermute(value, 'seq', [(source, source ^ 1) for source in range(128)])  2.67 us
    pallas_call x1, Pallas kernels, mix_all_call(): pl.pallas_call(mix_all_kernel, out_shape=jax.ShapeDtypeStruct((CLIPS, TOK...  2.11 us
    pallas_call x1, Pallas kernels, load_call(): pl.pallas_call(load_kernel, out_shape=jax.ShapeDtypeStruct((CLIPS, TOK, D...  1.8 us
  transfers between devices with their start and end apart: 16, of which 9 were waited for; matrix products, arithmetic and copies ran while one was open for 0% of the time, Pallas kernels for 6%

profile of v4, /device:TPU:1, one launch (start us, length us, event | category | flops | bytes accessed | tf_op | source)
XLA Modules:
  0.0 89.1 jit_solution(4156524830313664252)
XLA Ops:
  0.0 1.8 %load.1.x_ref = bf16[4,256,1280]{2,1,0:T(8,128)(2,1)S(1)} custom-call(bf16[4,256,1280]{2,1,0:T(8,128)(2,1)} %x_hbm.1), custom_call_target="tpu_custom_call" | custom-call | bytes 6291456 | tf_op jit(solution)/shard_map/load/pallas_call | solution.py:134
  1.9 3.4 %dispatch.1 = (bf16[64,2688]{1,0:T(8,128)(2,1)S(1)}, bf16[64,2688]{1,0:T(8,128)(2,1)S(1)}, bf16[64,2688]{1,0:T(8,128)(2,1)S(1)}, bf16[64,2688]{1,0:T(8,128)(2,1)...) custom-call(s32[18]{0:T(128)S(1)} %stack.63.where_ref, bf16[4,256,1280]{2,1,0:T(8,128)(2,1)S(1)} %load.1.x_ref, ...), custom_call_target="tpu_custom_call" | custom-call | flops 1006632960 | bytes 6291456 | tf_op jit(solution)/shard_map/dispatch/pallas_call | solution.py:178
  5.4 3.4 %collective-permute-start.1 = (bf16[64,2688]{1,0:T(8,128)(2,1)S(1)}, bf16[64,2688]{1,0:T(8,128)(2,1)S(1)}, u32[]{:S(2)}, u32[]{:S(2)}) collective-permute-start(bf16[64,2688]{1,0:T(8,128)(2,1)S(1)} %get-tuple-element.23.s3), channel_id=1, source_target_pairs={{0,1},{1,0},{2,3},{3,2},{4,5},{5,4},{6,7},{7,6},{8,9},{9,8},{10,11... | collective-permute-start | bytes 1032200 | tf_op jit(solution)/shard_map/ppermute | solution.py:54
  9.3 1.6 %own_half.1 = (f32[256,2560]{1,0:T(8,128)S(1)}, bf16[256,128]{1,0:T(8,128)(2,1)S(1)}) custom-call(s32[18]{0:T(128)S(1)} %stack.63.where_ref, bf16[4,256,1280]{2,1,0:T(8,128)(2,1)S(1)} %load.1.x_ref, bf16[256,1024]{1,0:T(8,128)(2,1)S(1)} %get-tuple-element.19.dispatch_ref, bf16[64,2688]{1,0:T(8,128)(2,1)S(1)} %get-tuple-element.20.s0, ...), custom_call_target="tpu_custom_call" | custom-call | flops 335544320 | bytes 6291456 | tf_op jit(solution)/shard_map/own_half/pallas_call | solution.py:207
  11.3 2.6 %collective-permute-start.2 = (bf16[64,2688]{1,0:T(8,128)(2,1)S(1)}, bf16[64,2688]{1,0:T(8,128)(2,1)S(1)}, u32[]{:S(2)}, u32[]{:S(2)}) collective-permute-start(bf16[64,2688]{1,0:T(8,128)(2,1)S(1)} %merge_cores.5), channel_id=1, source_target_pairs={{0,32},{1,67},{2,34},{3,65},{4,36},{5,71},{6,38},{7,69},{8,40},{9,... | collective-permute-start | bytes 1032200 | tf_op jit(solution)/shard_map/ppermute | solution.py:58
  14.7 1.7 %collective-permute-start.6 = (bf16[64,2688]{1,0:T(8,128)(2,1)S(1)}, bf16[64,2688]{1,0:T(8,128)(2,1)S(1)}, u32[]{:S(2)}, u32[]{:S(2)}) collective-permute-start(bf16[64,2688]{1,0:T(8,128)(2,1)S(1)} %merge_cores.7), channel_id=1, source_target_pairs={{0,48},{1,65},{2,50},{3,67},{4,52},{5,69},{6,54},{7,71},{8,56},{9,... | collective-permute-start | bytes 1032200 | tf_op jit(solution)/shard_map/ppermute | solution.py:58
  16.7 3.3 %collective-permute-done.2.refs_1_ = bf16[64,2688]{1,0:T(8,128)(2,1)S(1)} collective-permute-done((bf16[64,2688]{1,0:T(8,128)(2,1)S(1)}, bf16[64,2688]{1,0:T(8,128)(2,1)S(1)}, u32[]{:S(2)}, u32[]{:S(2)}) %collective-permute-start.2) | collective-permute-done | bytes 344096 | tf_op jit(solution)/shard_map/ppermute | solution.py:58
  20.0 2.4 %collective-permute-done.4.refs_2_ = bf16[64,2688]{1,0:T(8,128)(2,1)S(1)} collective-permute-done((bf16[64,2688]{1,0:T(8,128)(2,1)S(1)}, bf16[64,2688]{1,0:T(8,128)(2,1)S(1)}, u32[]{:S(2)}, u32[]{:S(2)}) %collective-permute-start.4) | collective-permute-done | bytes 344096 | tf_op jit(solution)/shard_map/ppermute | solution.py:58
  22.4 1.2 %collective-permute-done.6.refs_3_ = bf16[64,2688]{1,0:T(8,128)(2,1)S(1)} collective-permute-done((bf16[64,2688]{1,0:T(8,128)(2,1)S(1)}, bf16[64,2688]{1,0:T(8,128)(2,1)S(1)}, u32[]{:S(2)}, u32[]{:S(2)}) %collective-permute-start.6) | collective-permute-done | bytes 344096 | tf_op jit(solution)/shard_map/ppermute | solution.py:58
  23.6 0.6 merge_four.1
  24.2 22.8 %all_to_all.10.value_ref = bf16[16,4,2688]{2,1,0:T(4,128)(2,1)S(1)} all-to-all(bf16[16,4,2688]{2,1,0:T(4,128)(2,1)S(1)} %merge_four.1), channel_id=1, replica_groups={{0,2,4,6,8,10,12,14,64,66,68,70,72,74,76,78},{1,5,9,13,17,21,25,29,33,3..., dimensions={0} | all-to-all | bytes 688128 | tf_op jit(solution)/shard_map/all_to_all | solution.py:50
  47.3 1.4 %collective-permute-start.7 = (bf16[16,640]{1,0:T(8,128)(2,1)S(1)}, bf16[16,640]{1,0:T(8,128)(2,1)S(1)}, u32[]{:S(2)}, u32[]{:S(2)}) collective-permute-start(bf16[16,640]{1,0:T(8,128)(2,1)S(1)} %reshape.8.slot_in_ref), channel_id=1, source_target_pairs={{0,1},{1,0},{2,3},{3,2},{4,5},{5,4},{6,7},{7,6},{8,9},{9,8},{10,11... | collective-permute-start | bytes 61448 | tf_op jit(solution)/shard_map/ppermute | solution.py:54
  48.8 0.8 collective-permute-done.7.partner_ref
  49.6 1.1 %expert_in.1.hidden_ref = bf16[16,1280]{1,0:T(8,128)(2,1)S(1)} custom-call(s32[18]{0:T(128)S(1)} %stack.63.where_ref, bf16[16,640]{1,0:T(8,128)(2,1)S(1)} %reshape.8.slot_in_ref, bf16[16,640]{1,0:T(8,128)(2,1)S(1)} %collective-permute-done.7.partner_ref, bf16[1280,1280]{1,0:T(8,128)(2,1)S(1)} %copy-done, bf16[1,1280]{1,0:T(2,128)(2,1)S(1)} %broadcast_in_dim.10.b_ref), custom_call_target="tpu_custom_call" | custom-call | flops 52428800 | bytes 4194304 | tf_op jit(solution)/shard_map/expert_in/pallas_call | solution.py:259
  50.7 1.1 %expert_out.1 = (f32[16,640]{1,0:T(8,128)S(1)}, bf16[16,640]{1,0:T(8,128)(2,1)S(1)}) custom-call(s32[18]{0:T(128)S(1)} %stack.63.where_ref, bf16[16,1280]{1,0:T(8,128)(2,1)S(1)} %expert_in.1.hidden_ref, bf16[1280,1280]{1,0:T(8,128)(2,1)S(1)} %copy-done.1, bf16[64,1280]{1,0:T(8,128)(2,1)S(1)} %copy-done.4), custom_call_target="tpu_custom_call" | custom-call | flops 52428800 | bytes 4194304 | tf_op jit(solution)/shard_map/expert_out/pallas_call | solution.py:282
  52.3 0.8 collective-permute-done.8
  53.2 20.1 %all_to_all.11.value_ref = bf16[16,4,2560]{2,1,0:T(4,128)(2,1)S(1)} all-to-all(bf16[16,4,2560]{2,1,0:T(4,128)(2,1)S(1)} %broadcast_in_dim.12), channel_id=1, replica_groups={{0,2,4,6,8,10,12,14,64,66,68,70,72,74,76,78},{1,5,9,13,17,21,25,29,33,3..., dimensions={0} | all-to-all | bytes 655360 | tf_op jit(solution)/shard_map/all_to_all | solution.py:50
  74.2 3.5 %collective-permute-start.11 = (bf16[64,2560]{1,0:T(8,128)(2,1)S(1)}, bf16[64,2560]{1,0:T(8,128)(2,1)S(1)}, u32[]{:S(2)}, u32[]{:S(2)}) collective-permute-start(bf16[64,2560]{1,0:T(8,128)(2,1)S(1)} %flatten.1.piece_ref), channel_id=1, source_target_pairs={{0,32},{1,67},{2,34},{3,65},{4,36},{5,71},{6,38},{7,69},{8,40},{9,... | collective-permute-start | bytes 983048 | tf_op jit(solution)/shard_map/ppermute | solution.py:58
  77.7 1.5 %comb.1 = (bf16[4,256,256]{2,1,0:T(8,128)(2,1)S(1)}, bf16[4,256,256]{2,1,0:T(8,128)(2,1)S(1)}, bf16[64,2560]{1,0:T(8,128)(2,1)S(1)}) custom-call(s32[18]{0:T(128)S(1)} %stack.63.where_ref, f32[4,256,256]{2,1,0:T(8,128)S(1)} %copy-done.3, bf16[64,2560]{1,0:T(8,128)(2,1)S(1)} %flatten.1.piece_ref), custom_call_target="tpu_custom_call" | custom-call | flops 134217728 | bytes 4194304 | tf_op jit(solution)/shard_map/comb/pallas_call | solution.py:235
  79.8 5.0 %collective-permute-done.10.p2 = bf16[64,2560]{1,0:T(8,128)(2,1)S(1)} collective-permute-done((bf16[64,2560]{1,0:T(8,128)(2,1)S(1)}, bf16[64,2560]{1,0:T(8,128)(2,1)S(1)}, u32[]{:S(2)}, u32[]{:S(2)}) %collective-permute-start.10) | collective-permute-done | bytes 327712 | tf_op jit(solution)/shard_map/ppermute | solution.py:58
  84.7 0.5 collective-permute-start.15
  85.2 0.6 mix_own.1.own_ref
  85.8 0.5 collective-permute-done.14.p2
  86.8 2.1 %mix_all.1 = bf16[4,256,1280]{2,1,0:T(8,128)(2,1)} custom-call(s32[18]{0:T(128)S(1)} %stack.63.where_ref, bf16[4,256,640]{2,1,0:T(8,128)(2,1)S(1)} %mix_own.1.own_ref, bf16[4,256,256]{2,1,0:T(8,128)(2,1)S(1)} %get-tuple-element.30.comb_ref, bf16[64,2560]{1,0:T(8,128)(2,1)S(1)} %collective-permute-done.12.p0, ...), custom_call_target="tpu_custom_call" | custom-call | flops 335544320 | bytes 6291456 | tf_op jit(solution)/shard_map/mix_all/pallas_call | solution.py:450
  (45 shorter events, 4.9 us)
Async XLA Ops:
  0.0 1.9 %copy-start.5 = (bf16[1280,256]{1,0:T(8,128)(2,1)S(1)}, bf16[1280,256]{1,0:T(8,128)(2,1)}, u32[]{:S(2)}) copy-start(bf16[1280,256]{1,0:T(8,128)(2,1)} %phi_ref.1) | copy-start | bytes 1966084
  5.3 5.9 %copy-start.2 = (f32[4,256,256]{2,1,0:T(8,128)}, f32[4,256,256]{2,1,0:T(8,128)S(1)}, u32[]{:S(2)}) copy-start(f32[4,256,256]{2,1,0:T(8,128)S(1)} %get-tuple-element.18.logits_ref) | copy-start | bytes 3145732
  5.4 5.6 %collective-permute-start.1 = (bf16[64,2688]{1,0:T(8,128)(2,1)S(1)}, bf16[64,2688]{1,0:T(8,128)(2,1)S(1)}, u32[]{:S(2)}, u32[]{:S(2)}) collective-permute-start(bf16[64,2688]{1,0:T(8,128)(2,1)S(1)} %get-tuple-element.23.s3), channel_id=1, source_target_pairs={{0,1},{1,0},{2,3},{3,2},{4,5},{5,4},{6,7},{7,6},{8,9},{9,8},{10,11... | collective-permute-start | bytes 1032200 | tf_op jit(solution)/shard_map/ppermute | solution.py:54
  8.7 5.2 %collective-permute-start.3 = (bf16[64,2688]{1,0:T(8,128)(2,1)S(1)}, bf16[64,2688]{1,0:T(8,128)(2,1)S(1)}, u32[]{:S(2)}, u32[]{:S(2)}) collective-permute-start(bf16[64,2688]{1,0:T(8,128)(2,1)S(1)} %get-tuple-element.21.s1), channel_id=1, source_target_pairs={{0,1},{1,0},{2,3},{3,2},{4,5},{5,4},{6,7},{7,6},{8,9},{9,8},{10,11... | collective-permute-start | bytes 1032200 | tf_op jit(solution)/shard_map/ppermute | solution.py:54
  8.8 5.5 %collective-permute-start.5 = (bf16[64,2688]{1,0:T(8,128)(2,1)S(1)}, bf16[64,2688]{1,0:T(8,128)(2,1)S(1)}, u32[]{:S(2)}, u32[]{:S(2)}) collective-permute-start(bf16[64,2688]{1,0:T(8,128)(2,1)S(1)} %get-tuple-element.22.s2), channel_id=1, source_target_pairs={{0,1},{1,0},{2,3},{3,2},{4,5},{5,4},{6,7},{7,6},{8,9},{9,8},{10,11... | collective-permute-start | bytes 1032200 | tf_op jit(solution)/shard_map/ppermute | solution.py:54
  9.2 7.2 %collective-permute-start = (bf16[64,2688]{1,0:T(8,128)(2,1)S(1)}, bf16[64,2688]{1,0:T(8,128)(2,1)S(1)}, u32[]{:S(2)}, u32[]{:S(2)}) collective-permute-start(bf16[64,2688]{1,0:T(8,128)(2,1)S(1)} %get-tuple-element.20.s0), channel_id=1, source_target_pairs={{0,1},{1,0},{2,3},{3,2},{4,5},{5,4},{6,7},{7,6},{8,9},{9,8},{10,11... | collective-permute-start | bytes 1032200 | tf_op jit(solution)/shard_map/ppermute | solution.py:54
  11.3 8.7 %collective-permute-start.2 = (bf16[64,2688]{1,0:T(8,128)(2,1)S(1)}, bf16[64,2688]{1,0:T(8,128)(2,1)S(1)}, u32[]{:S(2)}, u32[]{:S(2)}) collective-permute-start(bf16[64,2688]{1,0:T(8,128)(2,1)S(1)} %merge_cores.5), channel_id=1, source_target_pairs={{0,32},{1,67},{2,34},{3,65},{4,36},{5,71},{6,38},{7,69},{8,40},{9,... | collective-permute-start | bytes 1032200 | tf_op jit(solution)/shard_map/ppermute | solution.py:58
  14.2 8.1 %collective-permute-start.4 = (bf16[64,2688]{1,0:T(8,128)(2,1)S(1)}, bf16[64,2688]{1,0:T(8,128)(2,1)S(1)}, u32[]{:S(2)}, u32[]{:S(2)}) collective-permute-start(bf16[64,2688]{1,0:T(8,128)(2,1)S(1)} %merge_cores.6), channel_id=1, source_target_pairs={{0,16},{1,3},{2,18},{3,1},{4,20},{5,7},{6,22},{7,5},{8,24},{9,11},... | collective-permute-start | bytes 1032200 | tf_op jit(solution)/shard_map/ppermute | solution.py:58
  14.7 34.1 %copy-start.6 = (bf16[1280]{0:T(1024)(128)(2,1)S(1)}, bf16[1280]{0:T(1024)(128)(2,1)}, u32[]{:S(2)}) copy-start(bf16[1280]{0:T(1024)(128)(2,1)} %param.9) | copy-start | bytes 7684
  14.7 34.9 %copy-start = (bf16[1280,1280]{1,0:T(8,128)(2,1)S(1)}, bf16[1280,1280]{1,0:T(8,128)(2,1)}, u32[]{:S(2)}) copy-start(bf16[1280,1280]{1,0:T(8,128)(2,1)} %w_ref.2) | copy-start | bytes 9830404
  14.7 8.9 %collective-permute-start.6 = (bf16[64,2688]{1,0:T(8,128)(2,1)S(1)}, bf16[64,2688]{1,0:T(8,128)(2,1)S(1)}, u32[]{:S(2)}, u32[]{:S(2)}) collective-permute-start(bf16[64,2688]{1,0:T(8,128)(2,1)S(1)} %merge_cores.7), channel_id=1, source_target_pairs={{0,48},{1,65},{2,50},{3,67},{4,52},{5,69},{6,54},{7,71},{8,56},{9,... | collective-permute-start | bytes 1032200 | tf_op jit(solution)/shard_map/ppermute | solution.py:58
  24.2 26.5 %copy-start.4 = (bf16[64,1280]{1,0:T(8,128)(2,1)S(1)}, bf16[64,1280]{1,0:T(8,128)(2,1)}, u32[]{:S(2)}) copy-start(bf16[64,1280]{1,0:T(8,128)(2,1)} %b_ref.1) | copy-start | bytes 491524
  47.3 3.4 %copy-start.1 = (bf16[1280,1280]{1,0:T(8,128)(2,1)S(1)}, bf16[1280,1280]{1,0:T(8,128)(2,1)}, u32[]{:S(2)}) copy-start(bf16[1280,1280]{1,0:T(8,128)(2,1)} %w_ref.3) | copy-start | bytes 9830404
  47.3 2.2 %collective-permute-start.7 = (bf16[16,640]{1,0:T(8,128)(2,1)S(1)}, bf16[16,640]{1,0:T(8,128)(2,1)S(1)}, u32[]{:S(2)}, u32[]{:S(2)}) collective-permute-start(bf16[16,640]{1,0:T(8,128)(2,1)S(1)} %reshape.8.slot_in_ref), channel_id=1, source_target_pairs={{0,1},{1,0},{2,3},{3,2},{4,5},{5,4},{6,7},{7,6},{8,9},{9,8},{10,11... | collective-permute-start | bytes 61448 | tf_op jit(solution)/shard_map/ppermute | solution.py:54
  50.7 26.9 %copy-start.3 = (f32[4,256,256]{2,1,0:T(8,128)S(1)}, f32[4,256,256]{2,1,0:T(8,128)}, u32[]{:S(2)}) copy-start(f32[4,256,256]{2,1,0:T(8,128)} %copy-done.2) | copy-start | bytes 3145732
  51.8 1.3 %collective-permute-start.8 = (bf16[16,640]{1,0:T(8,128)(2,1)S(1)}, bf16[16,640]{1,0:T(8,128)(2,1)S(1)}, u32[]{:S(2)}, u32[]{:S(2)}) collective-permute-start(bf16[16,640]{1,0:T(8,128)(2,1)S(1)} %get-tuple-element.27), channel_id=1, source_target_pairs={{0,1},{1,0},{2,3},{3,2},{4,5},{5,4},{6,7},{7,6},{8,9},{9,8},{10,11... | collective-permute-start | bytes 61448 | tf_op jit(solution)/shard_map/ppermute | solution.py:54
  73.4 6.0 %collective-permute-start.9 = (bf16[64,2560]{1,0:T(8,128)(2,1)S(1)}, bf16[64,2560]{1,0:T(8,128)(2,1)S(1)}, u32[]{:S(2)}, u32[]{:S(2)}) collective-permute-start(bf16[64,2560]{1,0:T(8,128)(2,1)S(1)} %flatten.1.piece_ref), channel_id=1, source_target_pairs={{0,16},{1,3},{2,18},{3,1},{4,20},{5,7},{6,22},{7,5},{8,24},{9,11},... | collective-permute-start | bytes 983048 | tf_op jit(solution)/shard_map/ppermute | solution.py:58
  73.8 10.9 %collective-permute-start.10 = (bf16[64,2560]{1,0:T(8,128)(2,1)S(1)}, bf16[64,2560]{1,0:T(8,128)(2,1)S(1)}, u32[]{:S(2)}, u32[]{:S(2)}) collective-permute-start(bf16[64,2560]{1,0:T(8,128)(2,1)S(1)} %flatten.1.piece_ref), channel_id=1, source_target_pairs={{0,48},{1,65},{2,50},{3,67},{4,52},{5,69},{6,54},{7,71},{8,56},{9,... | collective-permute-start | bytes 983048 | tf_op jit(solution)/shard_map/ppermute | solution.py:58
  74.2 10.6 %collective-permute-start.11 = (bf16[64,2560]{1,0:T(8,128)(2,1)S(1)}, bf16[64,2560]{1,0:T(8,128)(2,1)S(1)}, u32[]{:S(2)}, u32[]{:S(2)}) collective-permute-start(bf16[64,2560]{1,0:T(8,128)(2,1)S(1)} %flatten.1.piece_ref), channel_id=1, source_target_pairs={{0,32},{1,67},{2,34},{3,65},{4,36},{5,71},{6,38},{7,69},{8,40},{9,... | collective-permute-start | bytes 983048 | tf_op jit(solution)/shard_map/ppermute | solution.py:58
  79.2 6.7 %collective-permute-start.12 = (bf16[64,2560]{1,0:T(8,128)(2,1)S(1)}, bf16[64,2560]{1,0:T(8,128)(2,1)S(1)}, u32[]{:S(2)}, u32[]{:S(2)}) collective-permute-start(bf16[64,2560]{1,0:T(8,128)(2,1)S(1)} %get-tuple-element.29.p0), channel_id=1, source_target_pairs={{0,1},{1,0},{2,3},{3,2},{4,5},{5,4},{6,7},{7,6},{8,9},{9,8},{10,11... | collective-permute-start | bytes 983048 | tf_op jit(solution)/shard_map/ppermute | solution.py:54
  79.4 6.4 %collective-permute-start.13 = (bf16[64,2560]{1,0:T(8,128)(2,1)S(1)}, bf16[64,2560]{1,0:T(8,128)(2,1)S(1)}, u32[]{:S(2)}, u32[]{:S(2)}) collective-permute-start(bf16[64,2560]{1,0:T(8,128)(2,1)S(1)} %collective-permute-done.9.p1), channel_id=1, source_target_pairs={{0,1},{1,0},{2,3},{3,2},{4,5},{5,4},{6,7},{7,6},{8,9},{9,8},{10,11... | collective-permute-start | bytes 983048 | tf_op jit(solution)/shard_map/ppermute | solution.py:54
  84.7 1.6 %collective-permute-start.14 = (bf16[64,2560]{1,0:T(8,128)(2,1)S(1)}, bf16[64,2560]{1,0:T(8,128)(2,1)S(1)}, u32[]{:S(2)}, u32[]{:S(2)}) collective-permute-start(bf16[64,2560]{1,0:T(8,128)(2,1)S(1)} %collective-permute-done.10.p2), channel_id=1, source_target_pairs={{0,1},{1,0},{2,3},{3,2},{4,5},{5,4},{6,7},{7,6},{8,9},{9,8},{10,11... | collective-permute-start | bytes 983048 | tf_op jit(solution)/shard_map/ppermute | solution.py:54
  84.7 2.1 %collective-permute-start.15 = (bf16[64,2560]{1,0:T(8,128)(2,1)S(1)}, bf16[64,2560]{1,0:T(8,128)(2,1)S(1)}, u32[]{:S(2)}, u32[]{:S(2)}) collective-permute-start(bf16[64,2560]{1,0:T(8,128)(2,1)S(1)} %collective-permute-done.11.p3), channel_id=1, source_target_pairs={{0,1},{1,0},{2,3},{3,2},{4,5},{5,4},{6,7},{7,6},{8,9},{9,8},{10,11... | collective-permute-start | bytes 983048 | tf_op jit(solution)/shard_map/ppermute | solution.py:54

commit v5 on v4

--- a/solution.py
+++ b/solution.py
@@ -34,7 +34,15 @@
     return list(found.values())
 
 
-STAGE_TWO = groups_by(lambda y, x, z, core: (core, x) if core == 0 else (core, y, z % 2))
+def second_rank(index):
+    y, x, z, core = coords(index)
+    return z * 2 + y if core == 0 else z // 2 * 4 + x
+
+
+STAGE_TWO = [
+    sorted(group, key=second_rank)
+    for group in groups_by(lambda y, x, z, core: (core, x) if core == 0 else (core, y, z % 2))
+]
 
 
 def peer(index, k):
@@ -106,8 +114,8 @@
         jnp.where(k == 0, where_ref[start], where_ref[start + 1]),
         jnp.where(k == 2, where_ref[start + 2], where_ref[start + 3]),
     )
-    by_x = ((rest >> 5) << 7) | (piece << 5) | (rest & 31)
-    by_yz = ((piece >> 1) << 7) | ((rest >> 4) << 5) | (((rest >> 2) & 3) << 3) | ((piece & 1) << 2) | (rest & 3)
+    by_x = (((rest >> 2) & 1) << 7) | (piece << 5) | ((rest >> 3) << 2) | (rest & 3)
+    by_yz = ((piece >> 1) << 7) | (((rest >> 2) & 3) << 5) | ((rest >> 4) << 3) | ((piece & 1) << 2) | (rest & 3)
     slot = jnp.where(core == 0, by_x, by_yz)
     return jnp.where(lax.broadcasted_iota(jnp.int32, (SLOTS, SLOTS), 1) == slot, 1.0, 0.0).astype(BF16)
 
@@ -144,9 +152,12 @@
 
 
 def dispatch_kernel(where_ref, x_ref, phi_ref, *refs):
-    send_refs, (logits_ref, dispatch_ref) = refs[:4], refs[4:]
+    send_refs, (logits_ref, dispatch_ref, order_ref) = refs[:4], refs[4:]
     core = where_ref[0]
     order = order_matrix(1 - core, where_ref, OTHER_SENT)
+    order_ref[...] = lax.dot_general(
+        order_matrix(core, where_ref, SENT), order, (((1,), (1,)), ((), ())), preferred_element_type=F32
+    ).astype(BF16)
     tokens = x_ref[...].reshape(CLIPS * TOK, D)
     all_logits = jnp.dot(tokens, phi_ref[...], preferred_element_type=F32)
     stats = jnp.zeros((SLOTS, 128), F32)
@@ -181,20 +192,19 @@
         + (
             jax.ShapeDtypeStruct((CLIPS, TOK, SLOTS), F32),
             jax.ShapeDtypeStruct((SLOTS, CLIPS * TOK), BF16),
+            jax.ShapeDtypeStruct((SLOTS, SLOTS), BF16),
         ),
         in_specs=[SMEM_SPEC] + [VMEM_SPEC] * 2,
-        out_specs=(VMEM_SPEC,) * 6,
+        out_specs=(VMEM_SPEC,) * 7,
         compiler_params=params(DISPATCH_VMEM),
         cost_estimate=cost(2 * 1024 * 256 * 1920, 6 * 2**20),
         name="dispatch",
     )(where, x, slot_phi)
 
 
-def own_kernel(where_ref, x_ref, dispatch_ref, s0, s1, s2, s3, own_ref, stats_ref):
+def own_kernel(where_ref, x_ref, dispatch_ref, order_ref, s0, s1, s2, s3, own_ref, stats_ref):
     core = where_ref[0]
-    given = order_matrix(1 - core, where_ref, OTHER_SENT)
-    order = order_matrix(core, where_ref, SENT)
-    order = lax.dot_general(order, given, (((1,), (1,)), ((), ())), preferred_element_type=F32).astype(BF16)
+    order = order_ref[...]
     stats = jnp.concatenate([s[:, STATS:] for s in (s0, s1, s2, s3)], axis=0)
     stats_ref[...] = jnp.dot(order, stats, preferred_element_type=F32).astype(BF16)
     dispatch = jnp.dot(order, dispatch_ref[...], preferred_element_type=F32).astype(BF16)
@@ -203,19 +213,19 @@
         own_ref[:, column_slice(clip)] = jnp.dot(part, x_ref[clip, :, dynamic_half(core)], preferred_element_type=F32)
 
 
-def own_call(where, x, dispatch, sent):
+def own_call(where, x, dispatch, order, sent):
     return pl.pallas_call(
         own_kernel,
         out_shape=(
             jax.ShapeDtypeStruct((SLOTS, CLIPS * HALF), F32),
             jax.ShapeDtypeStruct((SLOTS, 128), BF16),
         ),
-        in_specs=[SMEM_SPEC] + [VMEM_SPEC] * 6,
+        in_specs=[SMEM_SPEC] + [VMEM_SPEC] * 7,
         out_specs=(VMEM_SPEC,) * 2,
         compiler_params=params(),
         cost_estimate=cost(2 * 1024 * 256 * 640, 6 * 2**20),
         name="own_half",
-    )(where, x, dispatch, *sent)
+    )(where, x, dispatch, order, *sent)
 
 
 def comb_kernel(where_ref, logits_ref, piece_ref, comb_ref, other_comb_ref, same_ref):
@@ -477,9 +487,9 @@
     other_to, other_got = targets(1 - core, y, x, z)
     where = jnp.stack([core] + to + other_to + got + other_got + [(me // 2).astype(jnp.int32)])
     tokens = load_call(clips_x)
-    *sent, logits, dispatch = dispatch_call(where, tokens, slot_phi)
+    *sent, logits, dispatch, order = dispatch_call(where, tokens, slot_phi)
     arrived = [swap_cores(piece) for piece in sent]
-    own, stats = own_call(where, tokens, dispatch, sent)
+    own, stats = own_call(where, tokens, dispatch, order, sent)
     pieces = [send_piece(merge_cores_call(k, own, stats, arrived[k]), k) for k in SEND_ORDER[:3]]
     packed = merge_four_call([merge_cores_call(0, own, stats, arrived[0])] + pieces)
     packed = exchange(packed, STAGE_TWO)

time: 89.3 us -> 89 us (level)
  starting transfers between devices: 15.3 us -> 19.4 us
  blocking collectives: 42.9 us -> 40.1 us
  waiting for transfers between devices: 14.7 us -> 13.4 us
    ppermute x10, starting transfers between devices: 6.73 us -> 10.6 us  [swap_cores(): lax.ppermute(value, 'seq', [(source, source ^ 1) for source in range(128)])]
    all_to_all x2, blocking collectives: 42.9 us -> 40.1 us  [exchange(): lax.all_to_all(value, 'seq', 0, 0, tiled=True, axis_index_groups=groups)]
    ppermute x6, waiting for transfers between devices: 12 us -> 10.9 us  [send_piece(): lax.ppermute(value, 'seq', [(source, peer(source, k)) for source in range...]
  transfers between devices with their start and end apart: 16 -> 16, of which waited for: 9 -> 9; matrix products, arithmetic and copies ran while one was open for 0% -> 0% of each run, Pallas kernels for 6% -> 5%
where the time goes in v5:
time: 89 us; the launch traced here: 88.8 us
  blocking collectives  40.1 us (45%)
  starting transfers between devices  19.4 us (22%)
  Pallas kernels  15.3 us (17%)
  waiting for transfers between devices  13.4 us (15%)
    all_to_all x2, blocking collectives, exchange(): lax.all_to_all(value, 'seq', 0, 0, tiled=True, axis_index_groups=groups)  40.1 us
    ppermute x6, waiting for transfers between devices, send_piece(): lax.ppermute(value, 'seq', [(source, peer(source, k)) for source in range...  10.9 us
    ppermute x10, starting transfers between devices, swap_cores(): lax.ppermute(value, 'seq', [(source, source ^ 1) for source in range(128)])  10.6 us
    ppermute x6, starting transfers between devices, send_piece(): lax.ppermute(value, 'seq', [(source, peer(source, k)) for source in range...  8.77 us
    pallas_call x1, Pallas kernels, dispatch_call(): pl.pallas_call(dispatch_kernel, out_shape=tuple((jax.ShapeDtypeStruct((64...  3.57 us
    ppermute x10, waiting for transfers between devices, swap_cores(): lax.ppermute(value, 'seq', [(source, source ^ 1) for source in range(128)])  2.47 us
    pallas_call x1, Pallas kernels, mix_all_call(): pl.pallas_call(mix_all_kernel, out_shape=jax.ShapeDtypeStruct((CLIPS, TOK...  2.11 us
    pallas_call x1, Pallas kernels, load_call(): pl.pallas_call(load_kernel, out_shape=jax.ShapeDtypeStruct((CLIPS, TOK, D...  1.8 us
  transfers between devices with their start and end apart: 16, of which 9 were waited for; matrix products, arithmetic and copies ran while one was open for 0% of the time, Pallas kernels for 5%

profile of v5, /device:TPU:1, one launch (start us, length us, event | category | flops | bytes accessed | tf_op | source)
XLA Modules:
  0.0 88.8 jit_solution(16067936950893835114)
XLA Ops:
  0.0 1.8 %load.1.x_ref = bf16[4,256,1280]{2,1,0:T(8,128)(2,1)S(1)} custom-call(bf16[4,256,1280]{2,1,0:T(8,128)(2,1)} %x_hbm.1), custom_call_target="tpu_custom_call" | custom-call | bytes 6291456 | tf_op jit(solution)/shard_map/load/pallas_call | solution.py:142
  1.9 3.6 %dispatch.1 = (bf16[64,2688]{1,0:T(8,128)(2,1)S(1)}, bf16[64,2688]{1,0:T(8,128)(2,1)S(1)}, bf16[64,2688]{1,0:T(8,128)(2,1)S(1)}, bf16[64,2688]{1,0:T(8,128)(2,1)...) custom-call(s32[18]{0:T(128)S(1)} %stack.63.where_ref, ...), custom_call_target="tpu_custom_call" | custom-call | flops 1006632960 | bytes 6291456 | tf_op jit(solution)/shard_map/dispatch/pallas_call | solution.py:189
  5.5 3.3 %collective-permute-start.1 = (bf16[64,2688]{1,0:T(8,128)(2,1)S(1)}, bf16[64,2688]{1,0:T(8,128)(2,1)S(1)}, u32[]{:S(2)}, u32[]{:S(2)}) collective-permute-start(bf16[64,2688]{1,0:T(8,128)(2,1)S(1)} %get-tuple-element.25.s3), channel_id=1, source_target_pairs={{0,1},{1,0},{2,3},{3,2},{4,5},{5,4},{6,7},{7,6},{8,9},{9,8},{10,11... | collective-permute-start | bytes 1032200 | tf_op jit(solution)/shard_map/ppermute | solution.py:62
  9.5 1.3 %own_half.1 = (f32[256,2560]{1,0:T(8,128)S(1)}, bf16[256,128]{1,0:T(8,128)(2,1)S(1)}) custom-call(s32[18]{0:T(128)S(1)} %stack.63.where_ref, bf16[4,256,1280]{2,1,0:T(8,128)(2,1)S(1)} %load.1.x_ref, bf16[256,1024]{1,0:T(8,128)(2,1)S(1)} %get-tuple-element.20.dispatch_ref, bf16[256,256]{1,0:T(8,128)(2,1)S(1)} %get-tuple-element.21.order_ref, ...), custom_call_target="tpu_custom_call" | custom-call | flops 335544320 | bytes 6291456 | tf_op jit(solution)/shard_map/own_half/pallas_call | solution.py:217
  11.1 2.6 %collective-permute-start.2 = (bf16[64,2688]{1,0:T(8,128)(2,1)S(1)}, bf16[64,2688]{1,0:T(8,128)(2,1)S(1)}, u32[]{:S(2)}, u32[]{:S(2)}) collective-permute-start(bf16[64,2688]{1,0:T(8,128)(2,1)S(1)} %merge_cores.5), channel_id=1, source_target_pairs={{0,32},{1,67},{2,34},{3,65},{4,36},{5,71},{6,38},{7,69},{8,40},{9,... | collective-permute-start | bytes 1032200 | tf_op jit(solution)/shard_map/ppermute | solution.py:66
  14.5 1.7 %collective-permute-start.6 = (bf16[64,2688]{1,0:T(8,128)(2,1)S(1)}, bf16[64,2688]{1,0:T(8,128)(2,1)S(1)}, u32[]{:S(2)}, u32[]{:S(2)}) collective-permute-start(bf16[64,2688]{1,0:T(8,128)(2,1)S(1)} %merge_cores.7), channel_id=1, source_target_pairs={{0,48},{1,65},{2,50},{3,67},{4,52},{5,69},{6,54},{7,71},{8,56},{9,... | collective-permute-start | bytes 1032200 | tf_op jit(solution)/shard_map/ppermute | solution.py:66
  16.5 3.3 %collective-permute-done.2.refs_1_ = bf16[64,2688]{1,0:T(8,128)(2,1)S(1)} collective-permute-done((bf16[64,2688]{1,0:T(8,128)(2,1)S(1)}, bf16[64,2688]{1,0:T(8,128)(2,1)S(1)}, u32[]{:S(2)}, u32[]{:S(2)}) %collective-permute-start.2) | collective-permute-done | bytes 344096 | tf_op jit(solution)/shard_map/ppermute | solution.py:66
  19.8 2.4 %collective-permute-done.4.refs_2_ = bf16[64,2688]{1,0:T(8,128)(2,1)S(1)} collective-permute-done((bf16[64,2688]{1,0:T(8,128)(2,1)S(1)}, bf16[64,2688]{1,0:T(8,128)(2,1)S(1)}, u32[]{:S(2)}, u32[]{:S(2)}) %collective-permute-start.4) | collective-permute-done | bytes 344096 | tf_op jit(solution)/shard_map/ppermute | solution.py:66
  22.2 1.2 %collective-permute-done.6.refs_3_ = bf16[64,2688]{1,0:T(8,128)(2,1)S(1)} collective-permute-done((bf16[64,2688]{1,0:T(8,128)(2,1)S(1)}, bf16[64,2688]{1,0:T(8,128)(2,1)S(1)}, u32[]{:S(2)}, u32[]{:S(2)}) %collective-permute-start.6) | collective-permute-done | bytes 344096 | tf_op jit(solution)/shard_map/ppermute | solution.py:66
  23.4 0.6 merge_four.1
  24.0 21.3 %all_to_all.10.value_ref = bf16[16,4,2688]{2,1,0:T(4,128)(2,1)S(1)} all-to-all(bf16[16,4,2688]{2,1,0:T(4,128)(2,1)S(1)} %merge_four.1), channel_id=1, replica_groups={{0,64,2,66,4,68,6,70,8,72,10,74,12,76,14,78},{1,17,33,49,5,21,37,53,9,2..., dimensions={0} | all-to-all | bytes 688128 | tf_op jit(solution)/shard_map/all_to_all | solution.py:58
  45.7 3.9 %collective-permute-start.7 = (bf16[16,640]{1,0:T(8,128)(2,1)S(1)}, bf16[16,640]{1,0:T(8,128)(2,1)S(1)}, u32[]{:S(2)}, u32[]{:S(2)}) collective-permute-start(bf16[16,640]{1,0:T(8,128)(2,1)S(1)} %reshape.8.slot_in_ref), channel_id=1, source_target_pairs={{0,1},{1,0},{2,3},{3,2},{4,5},{5,4},{6,7},{7,6},{8,9},{9,8},{10,11... | collective-permute-start | bytes 61448 | tf_op jit(solution)/shard_map/ppermute | solution.py:62
  49.6 0.8 collective-permute-done.7.partner_ref
  50.4 1.1 %expert_in.1.hidden_ref = bf16[16,1280]{1,0:T(8,128)(2,1)S(1)} custom-call(s32[18]{0:T(128)S(1)} %stack.63.where_ref, bf16[16,640]{1,0:T(8,128)(2,1)S(1)} %reshape.8.slot_in_ref, bf16[16,640]{1,0:T(8,128)(2,1)S(1)} %collective-permute-done.7.partner_ref, bf16[1280,1280]{1,0:T(8,128)(2,1)S(1)} %copy-done, bf16[1,1280]{1,0:T(2,128)(2,1)S(1)} %broadcast_in_dim.10.b_ref), custom_call_target="tpu_custom_call" | custom-call | flops 52428800 | bytes 4194304 | tf_op jit(solution)/shard_map/expert_in/pallas_call | solution.py:269
  51.6 1.1 %expert_out.1 = (f32[16,640]{1,0:T(8,128)S(1)}, bf16[16,640]{1,0:T(8,128)(2,1)S(1)}) custom-call(s32[18]{0:T(128)S(1)} %stack.63.where_ref, bf16[16,1280]{1,0:T(8,128)(2,1)S(1)} %expert_in.1.hidden_ref, bf16[1280,1280]{1,0:T(8,128)(2,1)S(1)} %copy-done.1, bf16[64,1280]{1,0:T(8,128)(2,1)S(1)} %copy-done.4), custom_call_target="tpu_custom_call" | custom-call | flops 52428800 | bytes 4194304 | tf_op jit(solution)/shard_map/expert_out/pallas_call | solution.py:292
  53.1 0.8 collective-permute-done.8
  54.1 18.7 %all_to_all.11.value_ref = bf16[16,4,2560]{2,1,0:T(4,128)(2,1)S(1)} all-to-all(bf16[16,4,2560]{2,1,0:T(4,128)(2,1)S(1)} %broadcast_in_dim.12), channel_id=1, replica_groups={{0,64,2,66,4,68,6,70,8,72,10,74,12,76,14,78},{1,17,33,49,5,21,37,53,9,2..., dimensions={0} | all-to-all | bytes 655360 | tf_op jit(solution)/shard_map/all_to_all | solution.py:58
  73.3 4.0 %collective-permute-start.11 = (bf16[64,2560]{1,0:T(8,128)(2,1)S(1)}, bf16[64,2560]{1,0:T(8,128)(2,1)S(1)}, u32[]{:S(2)}, u32[]{:S(2)}) collective-permute-start(bf16[64,2560]{1,0:T(8,128)(2,1)S(1)} %flatten.1.piece_ref), channel_id=1, source_target_pairs={{0,32},{1,67},{2,34},{3,65},{4,36},{5,71},{6,38},{7,69},{8,40},{9,... | collective-permute-start | bytes 983048 | tf_op jit(solution)/shard_map/ppermute | solution.py:66
  77.3 1.5 %comb.1 = (bf16[4,256,256]{2,1,0:T(8,128)(2,1)S(1)}, bf16[4,256,256]{2,1,0:T(8,128)(2,1)S(1)}, bf16[64,2560]{1,0:T(8,128)(2,1)S(1)}) custom-call(s32[18]{0:T(128)S(1)} %stack.63.where_ref, f32[4,256,256]{2,1,0:T(8,128)S(1)} %copy-done.3, bf16[64,2560]{1,0:T(8,128)(2,1)S(1)} %flatten.1.piece_ref), custom_call_target="tpu_custom_call" | custom-call | flops 134217728 | bytes 4194304 | tf_op jit(solution)/shard_map/comb/pallas_call | solution.py:245
  79.4 1.4 %collective-permute-start.13 = (bf16[64,2560]{1,0:T(8,128)(2,1)S(1)}, bf16[64,2560]{1,0:T(8,128)(2,1)S(1)}, u32[]{:S(2)}, u32[]{:S(2)}) collective-permute-start(bf16[64,2560]{1,0:T(8,128)(2,1)S(1)} %collective-permute-done.9.p1), channel_id=1, source_target_pairs={{0,1},{1,0},{2,3},{3,2},{4,5},{5,4},{6,7},{7,6},{8,9},{9,8},{10,11... | collective-permute-start | bytes 983048 | tf_op jit(solution)/shard_map/ppermute | solution.py:62
  80.7 3.7 %collective-permute-done.10.p2 = bf16[64,2560]{1,0:T(8,128)(2,1)S(1)} collective-permute-done((bf16[64,2560]{1,0:T(8,128)(2,1)S(1)}, bf16[64,2560]{1,0:T(8,128)(2,1)S(1)}, u32[]{:S(2)}, u32[]{:S(2)}) %collective-permute-start.10) | collective-permute-done | bytes 327712 | tf_op jit(solution)/shard_map/ppermute | solution.py:66
  84.5 0.7 collective-permute-start.15
  85.2 0.6 mix_own.1.own_ref
  86.6 2.1 %mix_all.1 = bf16[4,256,1280]{2,1,0:T(8,128)(2,1)} custom-call(s32[18]{0:T(128)S(1)} %stack.63.where_ref, bf16[4,256,640]{2,1,0:T(8,128)(2,1)S(1)} %mix_own.1.own_ref, bf16[4,256,256]{2,1,0:T(8,128)(2,1)S(1)} %get-tuple-element.32.comb_ref, bf16[64,2560]{1,0:T(8,128)(2,1)S(1)} %collective-permute-done.12.p0, ...), custom_call_target="tpu_custom_call" | custom-call | flops 335544320 | bytes 6291456 | tf_op jit(solution)/shard_map/mix_all/pallas_call | solution.py:460
  (45 shorter events, 4.8 us)
Async XLA Ops:
  0.0 1.9 %copy-start.5 = (bf16[1280,256]{1,0:T(8,128)(2,1)S(1)}, bf16[1280,256]{1,0:T(8,128)(2,1)}, u32[]{:S(2)}) copy-start(bf16[1280,256]{1,0:T(8,128)(2,1)} %phi_ref.1) | copy-start | bytes 1966084
  5.5 5.6 %copy-start.2 = (f32[4,256,256]{2,1,0:T(8,128)}, f32[4,256,256]{2,1,0:T(8,128)S(1)}, u32[]{:S(2)}) copy-start(f32[4,256,256]{2,1,0:T(8,128)S(1)} %get-tuple-element.19.logits_ref) | copy-start | bytes 3145732
  5.5 5.3 %collective-permute-start.1 = (bf16[64,2688]{1,0:T(8,128)(2,1)S(1)}, bf16[64,2688]{1,0:T(8,128)(2,1)S(1)}, u32[]{:S(2)}, u32[]{:S(2)}) collective-permute-start(bf16[64,2688]{1,0:T(8,128)(2,1)S(1)} %get-tuple-element.25.s3), channel_id=1, source_target_pairs={{0,1},{1,0},{2,3},{3,2},{4,5},{5,4},{6,7},{7,6},{8,9},{9,8},{10,11... | collective-permute-start | bytes 1032200 | tf_op jit(solution)/shard_map/ppermute | solution.py:62
  8.9 4.9 %collective-permute-start.3 = (bf16[64,2688]{1,0:T(8,128)(2,1)S(1)}, bf16[64,2688]{1,0:T(8,128)(2,1)S(1)}, u32[]{:S(2)}, u32[]{:S(2)}) collective-permute-start(bf16[64,2688]{1,0:T(8,128)(2,1)S(1)} %get-tuple-element.23.s1), channel_id=1, source_target_pairs={{0,1},{1,0},{2,3},{3,2},{4,5},{5,4},{6,7},{7,6},{8,9},{9,8},{10,11... | collective-permute-start | bytes 1032200 | tf_op jit(solution)/shard_map/ppermute | solution.py:62
  9.0 5.2 %collective-permute-start.5 = (bf16[64,2688]{1,0:T(8,128)(2,1)S(1)}, bf16[64,2688]{1,0:T(8,128)(2,1)S(1)}, u32[]{:S(2)}, u32[]{:S(2)}) collective-permute-start(bf16[64,2688]{1,0:T(8,128)(2,1)S(1)} %get-tuple-element.24.s2), channel_id=1, source_target_pairs={{0,1},{1,0},{2,3},{3,2},{4,5},{5,4},{6,7},{7,6},{8,9},{9,8},{10,11... | collective-permute-start | bytes 1032200 | tf_op jit(solution)/shard_map/ppermute | solution.py:62
  9.4 6.8 %collective-permute-start = (bf16[64,2688]{1,0:T(8,128)(2,1)S(1)}, bf16[64,2688]{1,0:T(8,128)(2,1)S(1)}, u32[]{:S(2)}, u32[]{:S(2)}) collective-permute-start(bf16[64,2688]{1,0:T(8,128)(2,1)S(1)} %get-tuple-element.22.s0), channel_id=1, source_target_pairs={{0,1},{1,0},{2,3},{3,2},{4,5},{5,4},{6,7},{7,6},{8,9},{9,8},{10,11... | collective-permute-start | bytes 1032200 | tf_op jit(solution)/shard_map/ppermute | solution.py:62
  11.1 8.7 %collective-permute-start.2 = (bf16[64,2688]{1,0:T(8,128)(2,1)S(1)}, bf16[64,2688]{1,0:T(8,128)(2,1)S(1)}, u32[]{:S(2)}, u32[]{:S(2)}) collective-permute-start(bf16[64,2688]{1,0:T(8,128)(2,1)S(1)} %merge_cores.5), channel_id=1, source_target_pairs={{0,32},{1,67},{2,34},{3,65},{4,36},{5,71},{6,38},{7,69},{8,40},{9,... | collective-permute-start | bytes 1032200 | tf_op jit(solution)/shard_map/ppermute | solution.py:66
  14.1 8.1 %collective-permute-start.4 = (bf16[64,2688]{1,0:T(8,128)(2,1)S(1)}, bf16[64,2688]{1,0:T(8,128)(2,1)S(1)}, u32[]{:S(2)}, u32[]{:S(2)}) collective-permute-start(bf16[64,2688]{1,0:T(8,128)(2,1)S(1)} %merge_cores.6), channel_id=1, source_target_pairs={{0,16},{1,3},{2,18},{3,1},{4,20},{5,7},{6,22},{7,5},{8,24},{9,11},... | collective-permute-start | bytes 1032200 | tf_op jit(solution)/shard_map/ppermute | solution.py:66
  14.5 35.1 %copy-start.6 = (bf16[1280]{0:T(1024)(128)(2,1)S(1)}, bf16[1280]{0:T(1024)(128)(2,1)}, u32[]{:S(2)}) copy-start(bf16[1280]{0:T(1024)(128)(2,1)} %param.9) | copy-start | bytes 7684
  14.5 35.9 %copy-start = (bf16[1280,1280]{1,0:T(8,128)(2,1)S(1)}, bf16[1280,1280]{1,0:T(8,128)(2,1)}, u32[]{:S(2)}) copy-start(bf16[1280,1280]{1,0:T(8,128)(2,1)} %w_ref.2) | copy-start | bytes 9830404
  14.5 8.9 %collective-permute-start.6 = (bf16[64,2688]{1,0:T(8,128)(2,1)S(1)}, bf16[64,2688]{1,0:T(8,128)(2,1)S(1)}, u32[]{:S(2)}, u32[]{:S(2)}) collective-permute-start(bf16[64,2688]{1,0:T(8,128)(2,1)S(1)} %merge_cores.7), channel_id=1, source_target_pairs={{0,48},{1,65},{2,50},{3,67},{4,52},{5,69},{6,54},{7,71},{8,56},{9,... | collective-permute-start | bytes 1032200 | tf_op jit(solution)/shard_map/ppermute | solution.py:66
  24.0 27.5 %copy-start.4 = (bf16[64,1280]{1,0:T(8,128)(2,1)S(1)}, bf16[64,1280]{1,0:T(8,128)(2,1)}, u32[]{:S(2)}) copy-start(bf16[64,1280]{1,0:T(8,128)(2,1)} %b_ref.1) | copy-start | bytes 491524
  45.7 5.8 %copy-start.1 = (bf16[1280,1280]{1,0:T(8,128)(2,1)S(1)}, bf16[1280,1280]{1,0:T(8,128)(2,1)}, u32[]{:S(2)}) copy-start(bf16[1280,1280]{1,0:T(8,128)(2,1)} %w_ref.3) | copy-start | bytes 9830404
  45.7 4.7 %collective-permute-start.7 = (bf16[16,640]{1,0:T(8,128)(2,1)S(1)}, bf16[16,640]{1,0:T(8,128)(2,1)S(1)}, u32[]{:S(2)}, u32[]{:S(2)}) collective-permute-start(bf16[16,640]{1,0:T(8,128)(2,1)S(1)} %reshape.8.slot_in_ref), channel_id=1, source_target_pairs={{0,1},{1,0},{2,3},{3,2},{4,5},{5,4},{6,7},{7,6},{8,9},{9,8},{10,11... | collective-permute-start | bytes 61448 | tf_op jit(solution)/shard_map/ppermute | solution.py:62
  51.6 25.8 %copy-start.3 = (f32[4,256,256]{2,1,0:T(8,128)S(1)}, f32[4,256,256]{2,1,0:T(8,128)}, u32[]{:S(2)}) copy-start(f32[4,256,256]{2,1,0:T(8,128)} %copy-done.2) | copy-start | bytes 3145732
  52.7 1.3 %collective-permute-start.8 = (bf16[16,640]{1,0:T(8,128)(2,1)S(1)}, bf16[16,640]{1,0:T(8,128)(2,1)S(1)}, u32[]{:S(2)}, u32[]{:S(2)}) collective-permute-start(bf16[16,640]{1,0:T(8,128)(2,1)S(1)} %get-tuple-element.29), channel_id=1, source_target_pairs={{0,1},{1,0},{2,3},{3,2},{4,5},{5,4},{6,7},{7,6},{8,9},{9,8},{10,11... | collective-permute-start | bytes 61448 | tf_op jit(solution)/shard_map/ppermute | solution.py:62
  72.9 6.5 %collective-permute-start.9 = (bf16[64,2560]{1,0:T(8,128)(2,1)S(1)}, bf16[64,2560]{1,0:T(8,128)(2,1)S(1)}, u32[]{:S(2)}, u32[]{:S(2)}) collective-permute-start(bf16[64,2560]{1,0:T(8,128)(2,1)S(1)} %flatten.1.piece_ref), channel_id=1, source_target_pairs={{0,16},{1,3},{2,18},{3,1},{4,20},{5,7},{6,22},{7,5},{8,24},{9,11},... | collective-permute-start | bytes 983048 | tf_op jit(solution)/shard_map/ppermute | solution.py:66
  73.2 11.3 %collective-permute-start.10 = (bf16[64,2560]{1,0:T(8,128)(2,1)S(1)}, bf16[64,2560]{1,0:T(8,128)(2,1)S(1)}, u32[]{:S(2)}, u32[]{:S(2)}) collective-permute-start(bf16[64,2560]{1,0:T(8,128)(2,1)S(1)} %flatten.1.piece_ref), channel_id=1, source_target_pairs={{0,48},{1,65},{2,50},{3,67},{4,52},{5,69},{6,54},{7,71},{8,56},{9,... | collective-permute-start | bytes 983048 | tf_op jit(solution)/shard_map/ppermute | solution.py:66
  73.3 11.2 %collective-permute-start.11 = (bf16[64,2560]{1,0:T(8,128)(2,1)S(1)}, bf16[64,2560]{1,0:T(8,128)(2,1)S(1)}, u32[]{:S(2)}, u32[]{:S(2)}) collective-permute-start(bf16[64,2560]{1,0:T(8,128)(2,1)S(1)} %flatten.1.piece_ref), channel_id=1, source_target_pairs={{0,32},{1,67},{2,34},{3,65},{4,36},{5,71},{6,38},{7,69},{8,40},{9,... | collective-permute-start | bytes 983048 | tf_op jit(solution)/shard_map/ppermute | solution.py:66
  78.8 7.0 %collective-permute-start.12 = (bf16[64,2560]{1,0:T(8,128)(2,1)S(1)}, bf16[64,2560]{1,0:T(8,128)(2,1)S(1)}, u32[]{:S(2)}, u32[]{:S(2)}) collective-permute-start(bf16[64,2560]{1,0:T(8,128)(2,1)S(1)} %get-tuple-element.31.p0), channel_id=1, source_target_pairs={{0,1},{1,0},{2,3},{3,2},{4,5},{5,4},{6,7},{7,6},{8,9},{9,8},{10,11... | collective-permute-start | bytes 983048 | tf_op jit(solution)/shard_map/ppermute | solution.py:62
  79.4 6.4 %collective-permute-start.13 = (bf16[64,2560]{1,0:T(8,128)(2,1)S(1)}, bf16[64,2560]{1,0:T(8,128)(2,1)S(1)}, u32[]{:S(2)}, u32[]{:S(2)}) collective-permute-start(bf16[64,2560]{1,0:T(8,128)(2,1)S(1)} %collective-permute-done.9.p1), channel_id=1, source_target_pairs={{0,1},{1,0},{2,3},{3,2},{4,5},{5,4},{6,7},{7,6},{8,9},{9,8},{10,11... | collective-permute-start | bytes 983048 | tf_op jit(solution)/shard_map/ppermute | solution.py:62
  84.5 1.6 %collective-permute-start.14 = (bf16[64,2560]{1,0:T(8,128)(2,1)S(1)}, bf16[64,2560]{1,0:T(8,128)(2,1)S(1)}, u32[]{:S(2)}, u32[]{:S(2)}) collective-permute-start(bf16[64,2560]{1,0:T(8,128)(2,1)S(1)} %collective-permute-done.10.p2), channel_id=1, source_target_pairs={{0,1},{1,0},{2,3},{3,2},{4,5},{5,4},{6,7},{7,6},{8,9},{9,8},{10,11... | collective-permute-start | bytes 983048 | tf_op jit(solution)/shard_map/ppermute | solution.py:62
  84.5 2.1 %collective-permute-start.15 = (bf16[64,2560]{1,0:T(8,128)(2,1)S(1)}, bf16[64,2560]{1,0:T(8,128)(2,1)S(1)}, u32[]{:S(2)}, u32[]{:S(2)}) collective-permute-start(bf16[64,2560]{1,0:T(8,128)(2,1)S(1)} %collective-permute-done.11.p3), channel_id=1, source_target_pairs={{0,1},{1,0},{2,3},{3,2},{4,5},{5,4},{6,7},{7,6},{8,9},{9,8},{10,11... | collective-permute-start | bytes 983048 | tf_op jit(solution)/shard_map/ppermute | solution.py:62
